TPU v7x, 512 devices: a whole 4x8x8 slice. The times are simulated.
512 devices in a mesh: gx: 16 (over y, core), gy: 32 (over z, x).
Axes of the slice: x: 4, y: 8, z: 8, core: 2. Of those that a mesh axis runs over, the one named last changes fastest.
Arguments:
- layer_input: bfloat16 [20, 128, 128, 1024], P(None, 'gx', 'gy'), may hold values from -6 to 6
- cotangent: bfloat16 [20, 128, 128, 1024], P(None, 'gx', 'gy'), may hold values from -6 to 6
- log_perm: float32 [128, 128, 64], P('gx', 'gy'), may hold values from -6 to 6
- well_cells: int32 [32], replicated, may hold values from 0 to 16383
- well_rates: int32 [32, 16], replicated, may hold values from 0 to 8
- inject_gain: float32 [2, 20], replicated, may hold values from -4 to 4
- spectral_weight: bfloat16 [2, 576, 144, 400], P(None, 'gy', 'gx'), may hold values from -12 to 12
- point_weight: bfloat16 [20, 20], replicated, may hold values from -1.25 to 1.25
- point_bias: float32 [20], replicated, may hold values from -3 to 3
Outputs:
- grad_input: bfloat16 [20, 128, 128, 1024], P(None, 'gx', 'gy')
- grad_spectral: float32 [2, 576, 144, 400], P(None, 'gy', 'gx')
- grad_perm: float32 [128, 128, 64], P('gx', 'gy')
Inputs may be any that keep to these rules, and one draw needn't show every extreme that they name: `well_cells`: several wells may share a column.
All inputs are finite; a program needn't handle non-finite values.
Results may differ from a plain program's by a relative error of at most 0.035.
Values may be sent and summed in bfloat16 or wider, within the bound.
A program may use at most 128 MiB of HBM per device.

v0:
```python
import math

import jax
import jax.numpy as jnp
from jax import lax
from jax.sharding import PartitionSpec as P

NX = 128
NY = 128
NZ = 64
NT = 16
MX = 24
MY = 24
MZ = 24
MT = 6


RATE_SCALE = 0.5
HIGH = lax.Precision.HIGHEST
INV_ROOT_TWO = 1.0 / math.sqrt(2.0)
INV_ROOT_TWO_PI = 1.0 / math.sqrt(2.0 * math.pi)


def signed_freq(index, count):
    return jnp.where(index < count // 2, index, index - count)


def wave_pair(count, length, cells):
    freq = signed_freq(jnp.arange(count, dtype=jnp.int32), count)
    turns = freq[:, None] * cells[None, :] % length
    angle = 2.0 * math.pi / length * turns.astype(jnp.float32)
    scale = 1.0 / math.sqrt(length)
    return (jnp.cos(angle) * scale, jnp.sin(angle) * scale)


def zt_tables():
    freq_z = signed_freq(jnp.arange(MZ, dtype=jnp.int32), MZ)
    freq_t = jnp.arange(MT, dtype=jnp.int32)
    depth = jnp.arange(NZ, dtype=jnp.int32)
    moment = jnp.arange(NT, dtype=jnp.int32)
    turns = (
        freq_z[:, None, None, None] * depth[None, None, :, None] * NT
        + freq_t[None, :, None, None] * moment[None, None, None, :] * NZ
    ) % (NZ * NT)
    angle = 2.0 * math.pi / (NZ * NT) * turns.reshape(MZ * MT, NZ * NT).astype(jnp.float32)
    scale = 1.0 / math.sqrt(NZ * NT)
    cosine = jnp.cos(angle) * scale
    sine = jnp.sin(angle) * scale
    weight = jnp.tile(jnp.where(freq_t == 0, 1.0, 2.0), MZ).astype(jnp.float32)
    forward = jnp.transpose(jnp.stack([cosine, -sine]), (2, 0, 1)).astype(jnp.bfloat16)
    inverse = jnp.stack([weight[:, None] * cosine, -weight[:, None] * sine]).astype(jnp.bfloat16)
    return (forward, inverse, weight)


def gelu_slope(value):
    return (
        0.5 * (1.0 + lax.erf(value * INV_ROOT_TWO))
        + value * jnp.exp(-0.5 * value * value) * INV_ROOT_TWO_PI
    )


def on_device(
    layer_input,
    cotangent,
    log_perm,
    well_cells,
    well_rates,
    inject_gain,
    spectral_weight,
    point_weight,
    point_bias,
):
    channels, x_cells, y_cells, zt_len = layer_input.shape
    flat = x_cells * y_cells
    y_devices = lax.axis_size("gy")
    m_local = MZ * MT // lax.axis_size("gx")
    mode_chan = m_local * channels
    rows_local = MX * MY // y_devices
    x_global = lax.axis_index("gx") * x_cells + jnp.arange(x_cells, dtype=jnp.int32)
    y_global = lax.axis_index("gy") * y_cells + jnp.arange(y_cells, dtype=jnp.int32)
    forward_zt, inverse_zt, mode_weight = zt_tables()
    cos_all, sin_all = wave_pair(MX, NX, jnp.arange(NX, dtype=jnp.int32))
    cos_narrow = cos_all.astype(jnp.bfloat16)
    sin_narrow = sin_all.astype(jnp.bfloat16)
    cos_y, sin_y = wave_pair(MY, NY, y_global)
    pair_ids = jnp.arange(channels * channels, dtype=jnp.int32)
    chan_ids = jnp.arange(channels, dtype=jnp.int32)
    sum_first = (pair_ids[:, None] % channels == chan_ids[None, :]).astype(jnp.float32)
    sum_second = (pair_ids[:, None] // channels == chan_ids[None, :]).astype(jnp.float32)
    cell_ids = (x_global[:, None] * NY + y_global[None, :]).reshape(flat)
    hits = (well_cells[:, None] == cell_ids[None, :]).astype(jnp.float32)
    inflow = RATE_SCALE * jnp.einsum(
        "wt,wa->at", well_rates.astype(jnp.float32), hits, precision=HIGH
    )
    perm_cols = jnp.repeat(log_perm.reshape(flat, NZ), NT, axis=1)
    flow_cols = jnp.tile(inflow, (1, NZ))
    lifted = (
        layer_input.astype(jnp.float32).reshape(channels, flat, zt_len)
        + inject_gain[0][:, None, None] * perm_cols[None, :, :]
        + inject_gain[1][:, None, None] * flow_cols[None, :, :]
    )
    lifted = lifted.astype(jnp.bfloat16)

    def spectra(field):
        field_cells = field.reshape(channels, x_cells, y_cells, zt_len)
        depth_spec = jnp.einsum(
            "cxyk,kpm->pyxmc", field_cells, forward_zt, preferred_element_type=jnp.float32
        ).astype(jnp.bfloat16)
        depth_spec = depth_spec.reshape(2, y_cells, x_cells, MZ * MT * channels)
        moved = lax.all_to_all(depth_spec, "gx", split_axis=3, concat_axis=2, tiled=True)
        even = jnp.einsum("jx,pyxq->pyjq", cos_narrow, moved, preferred_element_type=jnp.float32)
        odd = jnp.einsum("jx,pyxq->pyjq", sin_narrow, moved, preferred_element_type=jnp.float32)
        first = even[0] + odd[1]
        second = even[1] - odd[0]
        real = jnp.einsum("ky,yjq->jkq", cos_y, first, precision=HIGH) + jnp.einsum(
            "ky,yjq->jkq", sin_y, second, precision=HIGH
        )
        imag = jnp.einsum("ky,yjq->jkq", cos_y, second, precision=HIGH) - jnp.einsum(
            "ky,yjq->jkq", sin_y, first, precision=HIGH
        )
        term = jnp.stack([real, imag], axis=2).reshape(MX * MY, 2 * mode_chan)
        total = lax.psum(term.astype(jnp.bfloat16), "gy").astype(jnp.float32)
        mine = lax.dynamic_slice_in_dim(total, lax.axis_index("gy") * rows_local, rows_local, 0)
        return mine.reshape(rows_local, 2, mode_chan)

    def field_of(spec):
        piece = lax.all_gather(spec, "gy", axis=0, tiled=True)
        count = piece.shape[0]
        index = jnp.arange(count, dtype=jnp.int32)
        row_x = index // MY
        freq_y = signed_freq(index % MY, MY)
        pick = (row_x[:, None] == jnp.arange(MX, dtype=jnp.int32)[None, :]).astype(jnp.float32)
        angle = 2.0 * math.pi / NY * (freq_y[:, None] * y_global[None, :] % NY).astype(jnp.float32)
        scale = 1.0 / math.sqrt(NY)
        wave_cos = pick[:, :, None] * (jnp.cos(angle) * scale)[:, None, :]
        wave_sin = pick[:, :, None] * (jnp.sin(angle) * scale)[:, None, :]
        real = jnp.einsum("rjy,rq->yjq", wave_cos, piece[:, 0], precision=HIGH) - jnp.einsum(
            "rjy,rq->yjq", wave_sin, piece[:, 1], precision=HIGH
        )
        imag = jnp.einsum("rjy,rq->yjq", wave_cos, piece[:, 1], precision=HIGH) + jnp.einsum(
            "rjy,rq->yjq", wave_sin, piece[:, 0], precision=HIGH
        )
        partial_value = jnp.stack([real, imag])
        out_re = jnp.einsum("jx,yjq->yxq", cos_all, partial_value[0], precision=HIGH) - jnp.einsum(
            "jx,yjq->yxq", sin_all, partial_value[1], precision=HIGH
        )
        out_im = jnp.einsum("jx,yjq->yxq", cos_all, partial_value[1], precision=HIGH) + jnp.einsum(
            "jx,yjq->yxq", sin_all, partial_value[0], precision=HIGH
        )
        rows_out = jnp.stack([out_re, out_im]).astype(jnp.bfloat16)
        return lax.all_to_all(rows_out, "gx", split_axis=2, concat_axis=3, tiled=True)

    def to_field(image):
        modes = image.reshape(2, y_cells, x_cells, MZ * MT, channels)
        whole = jnp.einsum("pyxmc,pmk->cxyk", modes, inverse_zt, preferred_element_type=jnp.float32)
        return whole.reshape(channels, flat, zt_len)

    def spread_in(values):
        return jnp.repeat(values, channels, axis=2)

    def spread_out(values):
        return jnp.tile(values, (1, 1, channels))

    weight = spectral_weight.astype(jnp.float32)
    spec_in = spectra(lifted)
    lift_re = spec_in[:, 0].reshape(rows_local, m_local, channels)
    lift_im = spec_in[:, 1].reshape(rows_local, m_local, channels)
    mix_re = jnp.einsum(
        "rmq,qo->rmo",
        weight[0] * spread_in(lift_re) - weight[1] * spread_in(lift_im),
        sum_first,
        precision=HIGH,
    )
    mix_im = jnp.einsum(
        "rmq,qo->rmo",
        weight[0] * spread_in(lift_im) + weight[1] * spread_in(lift_re),
        sum_first,
        precision=HIGH,
    )
    mixed = jnp.stack([mix_re, mix_im], axis=1).reshape(rows_local, 2, mode_chan)
    image_field = to_field(field_of(mixed))
    pre = (
        image_field
        + jnp.einsum("co,cak->oak", point_weight, lifted, preferred_element_type=jnp.float32)
        + point_bias[:, None, None]
    )
    delta = (
        cotangent.astype(jnp.float32).reshape(channels, flat, zt_len) * gelu_slope(pre)
    ).astype(jnp.bfloat16)
    spec_delta = spectra(delta)
    delta_re = spec_delta[:, 0].reshape(rows_local, m_local, channels)
    delta_im = spec_delta[:, 1].reshape(rows_local, m_local, channels)
    kappa = lax.dynamic_slice_in_dim(mode_weight, lax.axis_index("gx") * m_local, m_local)[
        None, :, None
    ]
    grad_re = kappa * (
        spread_out(delta_re) * spread_in(lift_re) + spread_out(delta_im) * spread_in(lift_im)
    )
    grad_im = kappa * (
        spread_out(delta_im) * spread_in(lift_re) - spread_out(delta_re) * spread_in(lift_im)
    )
    grad_spectral = jnp.stack([grad_re, grad_im])
    back_re = jnp.einsum(
        "rmq,qc->rmc",
        weight[0] * spread_out(delta_re) + weight[1] * spread_out(delta_im),
        sum_second,
        precision=HIGH,
    )
    back_im = jnp.einsum(
        "rmq,qc->rmc",
        weight[0] * spread_out(delta_im) - weight[1] * spread_out(delta_re),
        sum_second,
        precision=HIGH,
    )
    back_spec = jnp.stack([back_re, back_im], axis=1).reshape(rows_local, 2, mode_chan)
    back_field = to_field(field_of(back_spec))
    grad_field = back_field + jnp.einsum(
        "co,oak->cak", point_weight, delta, preferred_element_type=jnp.float32
    )
    grad_input = grad_field.astype(jnp.bfloat16).reshape(channels, x_cells, y_cells, zt_len)
    per_cell = jnp.einsum("c,cak->ak", inject_gain[0], grad_field, precision=HIGH)
    grad_perm = jnp.sum(per_cell.reshape(x_cells, y_cells, NZ, NT), axis=3)
    return (grad_input, grad_spectral, grad_perm)


def solution(mesh):
    return jax.shard_map(
        on_device,
        mesh=mesh,
        in_specs=(
            P(None, "gx", "gy", None),
            P(None, "gx", "gy", None),
            P("gx", "gy", None),
            P(),
            P(),
            P(),
            P(None, "gy", "gx", None),
            P(),
            P(),
        ),
        out_specs=(P(None, "gx", "gy", None), P(None, "gy", "gx", None), P("gx", "gy", None)),
        check_vma=False,
    )
```

profile of v0, /device:TPU:1, one launch (start us, length us, event | category | flops | bytes accessed | tf_op | source)
XLA Modules:
  0.0 721.4 jit_solution(577773773620210356)
XLA Ops:
  10.9 2.8 broadcast_add_fusion
  13.7 5.1 add.347
  18.8 3.3 multiply_convert_fusion.2
  24.2 16.9 %copy.226 = bf16[2,4,8,144,20]{2,1,0,4,3:T(4,128)(2,1)} copy(bf16[2,4,8,144,20]{3,4,1,2,0:T(8,128)(2,1)S(1)} %fusion.16) | data formatting | bytes 737280 | tf_op jit(solution)/shard_map/reshape | solution.py:109
  41.2 13.6 %reshape.627 = bf16[16,2,5760]{2,1,0:T(2,128)(2,1)} reshape(bf16[2880,2,4,8]{3,2,1,0:T(4,128)(2,1)} %bitcast.321) | data formatting | bytes 737280
  54.8 10.2 %all-to-all-start = ((bf16[16,2,5760]{2,1,0:T(2,128)(2,1)}), bf16[16,2,5760]{2,1,0:T(2,128)(2,1)S(1)}, u32[]{:S(2)}, u32[]{:S(2)}) async-start(bf16[16,2,5760]{2,1,0:T(2,128)(2,1)} %reshape.627), calls=%async_computation | async-start | bytes 737280 | tf_op jit(solution)/shard_map/all_to_all | solution.py:110
  65.6 13.6 %all-to-all-done = bf16[16,2,5760]{2,1,0:T(2,128)(2,1)S(1)} async-done(((bf16[16,2,5760]{2,1,0:T(2,128)(2,1)}), bf16[16,2,5760]{2,1,0:T(2,128)(2,1)S(1)}, u32[]{:S(2)}, u32[]{:S(2)}) %all-to-all-start) | async-done | bytes 368672 | tf_op jit(solution)/shard_map/all_to_all | solution.py:110
  79.2 7.9 %reshape.628 = bf16[2880,2,4,8]{3,2,1,0:T(4,128)(2,1)} reshape(bf16[16,2,5760]{2,1,0:T(2,128)(2,1)S(1)} %all-to-all-done) | data formatting | bytes 737280
  87.1 6.6 copy.228
  99.8 152.1 %all-reduce.3.cloned.1.call-done = bf16[576,360]{1,0:T(8,128)(2,1)} async-done(((bf16[576,360]{1,0:T(8,128)(2,1)}), bf16[576,360]{1,0:T(8,128)(2,1)}) %all-reduce.3.cloned.1.call-update) | async-done | bytes 414736 | tf_op jit(solution)/shard_map/psum | solution.py:122
  253.7 1.3 reshape.585
  255.6 1.3 reshape.586
  256.9 1.6 fusion.74
  258.5 1.6 fusion.78
  260.5 37.5 %all_gather.6 = f32[576,2,180]{2,1,0:T(2,128)S(1)} all-gather(f32[18,2,180]{2,1,0:T(2,128)S(1)} %pad_maximum_fusion.5), channel_id=1, replica_groups=mesh['gx'=16,'gy'=32] {'gy'}, dimensions={0}, use_global_device_ids=true | all-gather | bytes 855360 | tf_op jit(solution)/shard_map/all_gather | solution.py:127
  307.9 23.7 %all-to-all-start.1 = ((bf16[2,4,128,180]{3,1,0,2:T(4,128)(2,1)}), bf16[2,4,128,180]{3,1,0,2:T(4,128)(2,1)}, u32[]{:S(2)}, u32[]{:S(2)}) async-start(bf16[2,4,128,180]{3,1,0,2:T(4,128)(2,1)} %copy.172), calls=%async_computation.1 | async-start | bytes 1048576 | tf_op jit(solution)/shard_map/all_to_all | solution.py:151
  332.0 2.1 copy.231
  334.9 1.9 copy.177
  337.6 1.9 copy.179
  339.5 3.8 copy.148
  343.3 1.9 fusion.8
  345.2 3.9 all-to-all-done.1
  350.3 2.1 reshape.621
  352.5 2.5 convolution_bitcast_fusion.1
  355.4 1.4 copy-done.4
  357.3 2.4 fusion.5
  361.9 16.9 %copy.233 = bf16[2,4,8,144,20]{2,1,0,4,3:T(4,128)(2,1)} copy(bf16[2,4,8,144,20]{3,4,1,2,0:T(8,128)(2,1)S(1)} %fusion.15) | data formatting | bytes 737280 | tf_op jit(solution)/shard_map/reshape | solution.py:109
  378.8 13.0 %reshape.629 = bf16[16,2,5760]{2,1,0:T(2,128)(2,1)S(1)} reshape(bf16[2880,2,4,8]{3,2,1,0:T(4,128)(2,1)} %bitcast.323) | data formatting | bytes 737280
  391.8 17.4 %all_to_all.66 = bf16[16,2,5760]{2,1,0:T(2,128)(2,1)S(1)} all-to-all(bf16[16,2,5760]{2,1,0:T(2,128)(2,1)S(1)} %reshape.629), channel_id=1, replica_groups=mesh['gx'=16,'gy'=32] {'gx'}, dimensions={0} | all-to-all | bytes 737280 | tf_op jit(solution)/shard_map/all_to_all | solution.py:110
  409.2 7.9 %reshape.630 = bf16[2880,2,4,8]{3,2,1,0:T(4,128)(2,1)} reshape(bf16[16,2,5760]{2,1,0:T(2,128)(2,1)S(1)} %all_to_all.66) | data formatting | bytes 737280
  417.1 6.6 copy.235
  429.6 146.8 %all-reduce.5.cloned.1.call-done = bf16[576,360]{1,0:T(8,128)(2,1)} async-done(((bf16[576,360]{1,0:T(8,128)(2,1)}), bf16[576,360]{1,0:T(8,128)(2,1)}) %all-reduce.5.cloned.1.call-update) | async-done | bytes 414736 | tf_op jit(solution)/shard_map/psum | solution.py:122
  577.7 1.3 tile.27
  579.2 1.3 tile.30
  580.6 1.6 fusion.66
  582.1 1.6 fusion.70
  584.1 37.8 %all_gather.7 = f32[576,2,180]{2,1,0:T(2,128)S(1)} all-gather(f32[18,2,180]{2,1,0:T(2,128)S(1)} %pad_maximum_fusion.6), channel_id=1, replica_groups=mesh['gx'=16,'gy'=32] {'gy'}, dimensions={0}, use_global_device_ids=true | all-gather | bytes 855360 | tf_op jit(solution)/shard_map/all_gather | solution.py:127
  631.8 24.0 %all-to-all-start.3 = ((bf16[2,4,128,180]{3,1,0,2:T(4,128)(2,1)}), bf16[2,4,128,180]{3,1,0,2:T(4,128)(2,1)S(1)}, u32[]{:S(2)}, u32[]{:S(2)}) async-start(bf16[2,4,128,180]{3,1,0,2:T(4,128)(2,1)} %copy.201), calls=%async_computation.3 | async-start | bytes 1048576 | tf_op jit(solution)/shard_map/all_to_all | solution.py:151
  655.8 2.6 multiply_add_fusion
  658.4 2.1 add.394
  661.4 1.4 copy.209
  662.7 10.3 %all-to-all-done.3 = bf16[2,4,128,180]{3,1,0,2:T(4,128)(2,1)S(1)} async-done(((bf16[2,4,128,180]{3,1,0,2:T(4,128)(2,1)}), bf16[2,4,128,180]{3,1,0,2:T(4,128)(2,1)S(1)}, u32[]{:S(2)}, u32[]{:S(2)}) %all-to-all-start.3) | async-done | bytes 368672 | tf_op jit(solution)/shard_map/all_to_all | solution.py:151
  673.2 2.1 reshape.622
  675.4 1.4 convolution_bitcast_fusion
  679.0 2.1 copy.208
  681.1 10.6 %reshape.620 = f32[8,4,64,16,20]{3,2,4,1,0:T(8,128)} reshape(f32[32,1024,20]{1,2,0:T(8,128)S(1)} %bitcast.325) | data formatting | bytes 5242880 | tf_op jit(solution)/shard_map/c,cak->ak/dot_general | solution.py:221
  691.6 16.1 %copy.223 = f32[8,4,64,16,20]{2,4,3,1,0:T(8,128)} copy(f32[8,4,64,16,20]{3,2,4,1,0:T(8,128)} %reshape.620) | data formatting | bytes 5242880 | tf_op jit(solution)/shard_map/c,cak->ak/dot_general | solution.py:221
  707.7 6.0 fusion.201
  (160 shorter events, 52.3 us)
Async XLA Ops:
  7.2 348.2 %copy-start = (bf16[20,20]{1,0:T(8,128)(2,1)S(1)}, bf16[20,20]{1,0:T(8,128)(2,1)}, u32[]{:S(2)}) copy-start(bf16[20,20]{1,0:T(8,128)(2,1)} %param.16) | copy-start | bytes 2404
  7.2 2.8 copy-start.17
  13.7 8.4 %copy-start.3 = (bf16[20,8,4,1024]{3,2,1,0:T(4,128)(2,1)S(1)}, bf16[20,8,4,1024]{3,2,1,0:T(4,128)(2,1)}, u32[]{:S(2)}) copy-start(bf16[20,8,4,1024]{3,2,1,0:T(4,128)(2,1)} %param.9) | copy-start | bytes 3932164
  22.0 1.1 copy-start.13
  22.0 1.1 copy-start.15
  54.8 24.4 %all-to-all-start = ((bf16[16,2,5760]{2,1,0:T(2,128)(2,1)}), bf16[16,2,5760]{2,1,0:T(2,128)(2,1)S(1)}, u32[]{:S(2)}, u32[]{:S(2)}) async-start(bf16[16,2,5760]{2,1,0:T(2,128)(2,1)} %reshape.627), calls=%async_computation | async-start | bytes 737280 | tf_op jit(solution)/shard_map/all_to_all | solution.py:110
  65.0 186.8 %all-reduce.3.cloned.1.call-start = ((), (), s32[]{:S(2)}) async-start(), calls=%async_computation.4 | async-start | bytes 884736 | tf_op jit(solution)/shard_map/psum | solution.py:122
  96.8 2.9 copy-start.10
  99.8 158.7 %copy-start.1 = (f32[2,18,9,400]{3,1,2,0:T(8,128)}, f32[2,18,9,400]{3,1,2,0:T(8,128)S(1)}, u32[]{:S(2)}) copy-start(f32[2,18,9,400]{3,1,2,0:T(8,128)S(1)} %copy_convert_fusion) | copy-start | bytes 1555204
  307.9 41.2 %all-to-all-start.1 = ((bf16[2,4,128,180]{3,1,0,2:T(4,128)(2,1)}), bf16[2,4,128,180]{3,1,0,2:T(4,128)(2,1)}, u32[]{:S(2)}, u32[]{:S(2)}) async-start(bf16[2,4,128,180]{3,1,0,2:T(4,128)(2,1)} %copy.172), calls=%async_computation.1 | async-start | bytes 1048576 | tf_op jit(solution)/shard_map/all_to_all | solution.py:151
  331.6 244.8 %all-reduce.5.cloned.1.call-start = ((), (), s32[]{:S(2)}) async-start(), calls=%async_computation.5 | async-start | bytes 884736 | tf_op jit(solution)/shard_map/psum | solution.py:122
  339.5 3.8 copy-start.8
  339.5 3.8 copy-start.9
  354.9 1.9 copy-start.4
  355.0 2.3 copy-start.7
  355.0 2.3 copy-start.19
  357.3 3.6 copy-start.14
  357.3 3.6 copy-start.16
  359.7 1.1 copy-start.5
  579.1 1.5 copy-start.2
  631.8 41.2 %all-to-all-start.3 = ((bf16[2,4,128,180]{3,1,0,2:T(4,128)(2,1)}), bf16[2,4,128,180]{3,1,0,2:T(4,128)(2,1)S(1)}, u32[]{:S(2)}, u32[]{:S(2)}) async-start(bf16[2,4,128,180]{3,1,0,2:T(4,128)(2,1)} %copy.201), calls=%async_computation.3 | async-start | bytes 1048576 | tf_op jit(solution)/shard_map/all_to_all | solution.py:151
  662.7 12.7 %copy-start.11 = (bf16[1,144,1024]{2,1,0:T(8,128)(2,1)S(1)}, bf16[1,144,1024]{2,1,0:T(8,128)(2,1)}, u32[]{:S(2)}) copy-start(bf16[1,144,1024]{2,1,0:T(8,128)(2,1)} %get-tuple-element.23) | copy-start | bytes 884740
  662.7 12.7 %copy-start.12 = (bf16[1,144,1024]{2,1,0:T(8,128)(2,1)S(1)}, bf16[1,144,1024]{2,1,0:T(8,128)(2,1)}, u32[]{:S(2)}) copy-start(bf16[1,144,1024]{2,1,0:T(8,128)(2,1)} %get-tuple-element.26) | copy-start | bytes 884740
  676.8 1.4 copy-start.6
  691.6 16.1 %copy-start.18 = (f32[2,20]{1,0:T(2,128)S(1)}, f32[2,20]{1,0:T(2,128)}, u32[]{:S(2)}) copy-start(f32[2,20]{1,0:T(2,128)} %param.14) | copy-start | bytes 484
Sparse Core Ops, SparseCore 0:
  99.6 152.2 all-reduce.2
  429.6 146.7 all-reduce.4
where the time goes:
time: 731 us; the launch traced here: 721 us
  waiting for transfers between devices  327 us (45%)
  local copies, waits for them, and re-layouts  171 us (23%)
  blocking collectives  92.7 us (13%)
  starting transfers between devices  58.7 us (8%)
  matrix products  41.8 us (6%)
  between operations  15.2 us (2%)
  other arithmetic  14.9 us (2%)
    psum x2, waiting for transfers between devices, spectra(): total = lax.psum(term.astype(jnp.bfloat16), 'gy').astype(jnp.float32)  299 us
    all_gather x2, blocking collectives, field_of(): piece = lax.all_gather(spec, 'gy', axis=0, tiled=True)  75.3 us
    unnamed x51, local copies, waits for them, and re-layouts  53.6 us
    all_to_all x2, starting transfers between devices, field_of(): lax.all_to_all(rows_out, 'gx', split_axis=2, concat_axis=3, tiled=True)  47.7 us
    reshape x2, local copies, waits for them, and re-layouts, spectra(): depth_spec = depth_spec.reshape(2, y_cells, x_cells, MZ * MT * channels)  33.8 us
    dot_general x2, local copies, waits for them, and re-layouts, on_device(): jnp.einsum('c,cak->ak', inject_gain[0], grad_field, precision=HIGH)  26.6 us
    all_to_all x1, blocking collectives, spectra(): lax.all_to_all(depth_spec, 'gx', split_axis=3, concat_axis=2, tiled=True)  17.4 us
  transfers between devices with their start and end apart: 5, of which 5 were waited for; matrix products, arithmetic and copies ran while one was open for 3% of the time, Pallas kernels for 0%

commit v1 on v0

v1 whole, which is shorter than its diff:
```python
import math

import jax
import jax.numpy as jnp
import ml_dtypes
import numpy as np
from jax import lax
from jax.experimental import pallas as pl
from jax.experimental.pallas import tpu as pltpu
from jax.sharding import PartitionSpec as P

C = 20
NX, NY, NZ, NT = 128, 128, 64, 16
MX, MY, MZ, MT = 24, 24, 24, 6
GX, GY = 16, 32
XL, YL = NX // GX, NY // GY
ML = MZ * MT // GX
RL = MX * MY // GY
ZT = NZ * NT
CY = C * YL
NMODE = 2 * MZ * MT
LANES = 768
RB = 384
BF = jnp.bfloat16
F32 = jnp.float32
MESH = pl.DeviceIdType.MESH
INV_ROOT_TWO = 1.0 / math.sqrt(2.0)
INV_ROOT_TWO_PI = 1.0 / math.sqrt(2.0 * math.pi)


def freq(j, n):
    return np.where(j < n // 2, j, j - n)


def lane_of(m, cy):
    if m < 6:
        return m * 128 + cy
    if cy < 48:
        return (m - 6) * 128 + 80 + cy
    return (m - 3) * 128 + 80 + cy - 48


def first_jx(d):
    return 3 * d // 4


def tables():
    jz, jt = np.divmod(np.arange(MZ * MT), MT)
    k = np.arange(ZT)
    turns = (freq(jz, MZ)[:, None] * (k // NT)[None] * NT + jt[:, None] * (k % NT)[None] * NZ) % ZT
    ang = 2 * np.pi / ZT * turns
    cos, sin = np.cos(ang) / math.sqrt(ZT), np.sin(ang) / math.sqrt(ZT)
    kap = np.where(jt == 0, 1.0, 2.0)[:, None]
    ft = np.stack([cos, -sin], 1).reshape(NMODE, ZT)
    inv = np.stack([kap * cos, -kap * sin], 1).reshape(NMODE, ZT)
    jx = np.arange(MX)
    ang = 2 * np.pi / NX * (freq(jx, MX)[:, None] * np.arange(NX)[None] % NX)
    cx = (np.cos(ang) / math.sqrt(NX)).reshape(MX, GX, XL)
    sx = (np.sin(ang) / math.sqrt(NX)).reshape(MX, GX, XL)
    wx = np.zeros((MX, 2, GX, 2, XL))
    wx[:, 0, :, 0], wx[:, 0, :, 1] = cx, sx
    wx[:, 1, :, 1], wx[:, 1, :, 0] = cx, -sx
    wx = wx.reshape(2 * MX, 2 * NX)
    xi = np.zeros((2 * NX, 128))
    xi[:, : 2 * MX] = wx.T
    perm = np.zeros((LANES, YL * 256))
    for m in range(ML):
        for c in range(C):
            for y in range(YL):
                perm[lane_of(m, c * YL + y), y * 256 + m * C + c] = 1
    pick = np.zeros((GY, YL, 2, 2, YL, MX, 2))
    for d in range(GY):
        for s in range(2):
            if s == 1 and d % 4 in (0, 3):
                continue
            for y in range(YL):
                for p in range(2):
                    pick[d, y, s, p, y, first_jx(d) + s, p] = 1
    pick = pick.reshape(GY * 16, YL * MX * 2)
    pick_pad = np.zeros((GY * 16, 256))
    pick_pad[:, : YL * MX * 2] = pick
    vc = np.zeros((GY, RL, 2, GY, YL, 2, 2))
    for d in range(GY):
        for i in range(RL):
            a, b = divmod(d * RL + i, MY)
            ang = 2 * np.pi / NY * (int(freq(np.array(b), MY)) * np.arange(NY) % NY)
            cy = (np.cos(ang) / math.sqrt(NY)).reshape(GY, YL)
            sy = (np.sin(ang) / math.sqrt(NY)).reshape(GY, YL)
            s = a - first_jx(d)
            vc[d, i, 0, :, :, s, 0], vc[d, i, 0, :, :, s, 1] = cy, sy
            vc[d, i, 1, :, :, s, 1], vc[d, i, 1, :, :, s, 0] = cy, -sy
    vc = vc.reshape(GY, 2 * RL, GY * 16)
    v_pad = np.zeros((GY, 48, GY * 16))
    v_pad[:, : 2 * RL] = vc
    u_pad = np.zeros((GY, GY * 16, 128))
    u_pad[:, :, : 2 * RL] = vc.transpose(0, 2, 1)
    rep = np.zeros((6, RB, 128))
    forms = [
        ((0, 1), (1, -1)),
        ((1, 1), (0, 1)),
        ((0, 1), (1, 1)),
        ((1, 1), (0, -1)),
        ((0, 1), (0, 1)),
        ((1, 1), (1, 1)),
    ]
    back = np.zeros((48, 2, RB))
    mask = np.zeros((RB, 256))
    kmask = np.zeros((2, RB, 256))
    for r in range(RL):
        for m in range(ML):
            for p in range(2):
                row = (r * ML + m) * 2 + p
                for f, form in enumerate(forms):
                    rep[f, row, 2 * r + form[p][0]] = form[p][1]
                back[2 * r, 0, row] = 1
                back[2 * r + 1, 1, row] = 1
                mask[row, m * C : (m + 1) * C] = 1
                for g in range(2):
                    kmask[g, row, m * C : (m + 1) * C] = 1 if (ML * g + m) % MT == 0 else 2
    spread = np.zeros((2, 256, 512))
    for m in range(ML):
        for c in range(C):
            for o in range(C):
                spread[0, m * C + c, c * C + o] = 1
                spread[1, m * C + o, c * C + o] = 1
    cell = np.zeros((XL, C, YL, XL, YL))
    for x in range(XL):
        for y in range(YL):
            cell[x, :, y, x, y] = 1
    cell = cell.reshape(XL * CY, XL * YL)
    chan = np.zeros((CY, C))
    chan[np.arange(CY), np.arange(CY) // YL] = 1
    chan_t = np.zeros((C, 128))
    chan_t[:, :CY] = chan.T
    same_y = np.zeros((CY, 128))
    same_y[:, :CY] = np.arange(CY)[:, None] % YL == np.arange(CY)[None] % YL
    ztrep = np.zeros((NZ + NT, ZT))
    ztrep[k // NT, k] = 1
    ztrep[NZ + k % NT, k] = 1
    zsum = np.zeros((ZT, 128))
    zsum[k, k // NT] = 1
    out = dict(
        ft=ft, inv=inv, wx=wx, xi=xi, perm=perm, perm_t=perm.T, pick=pick_pad, sel=pick.T,
        v=v_pad, u=u_pad, rep=rep.reshape(6 * RB, 128), back=back.reshape(48, 2 * RB),
        mask=mask, kmask=kmask, spread1=spread[0], spread2=spread[1],
        sum1=spread[1].T, sum2=spread[0].T, cell=cell, chan=chan, chan_t=chan_t,
        same_y=same_y, ztrep=ztrep, zsum=zsum,
    )
    return {n: np.ascontiguousarray(a).astype(ml_dtypes.bfloat16) for n, a in out.items()}


TABLE_ORDER = (
    "cell", "chan", "ztrep", "ft", "chan_t", "same_y", "wx", "perm", "pick", "v", "rep", "mask",
    "spread1", "sum1", "back", "u", "sel", "perm_t", "xi", "inv", "kmask", "spread2", "sum2", "zsum",
)
OWN = {"v": 32, "u": 32, "kmask": 2}


def dot(a, b):
    return lax.dot_general(a, b, (((1,), (0,)), ((), ())), preferred_element_type=F32)


def dot_nt(a, b):
    return lax.dot_general(a, b, (((1,), (1,)), ((), ())), preferred_element_type=F32)


def dot_tn(a, b):
    return lax.dot_general(a, b, (((0,), (0,)), ((), ())), preferred_element_type=F32)


def gelu_slope(v):
    a = jnp.abs(v) * INV_ROOT_TWO
    t = 1.0 / (1.0 + 0.3275911 * a)
    poly = t * (
        0.254829592
        + t * (-0.284496736 + t * (1.421413741 + t * (-1.453152027 + t * 1.061405429)))
    )
    e = jnp.exp(-0.5 * v * v)
    tail = 0.5 * poly * e
    return jnp.where(v >= 0, 1.0 - tail, tail) + v * e * INV_ROOT_TWO_PI


def split(a):
    hi = a.astype(BF)
    return hi, (a - hi.astype(F32)).astype(BF)


def kernel(*refs):
    names = TABLE_ORDER
    (x_hbm, cot_hbm, w_hbm, perm_ref, cells_ref, rates_ref, gain_ref, pw_ref, bias_ref) = refs[:9]
    hbm = dict(zip(names, refs[9 : 9 + len(names)]))
    pos = 9 + len(names)
    out_hbm, gs_hbm, gp_ref = refs[pos : pos + 3]
    pos += 3
    (
        x_v, cot_v, w_v, out_v, gs_v, lbf, base, cotf, wf, perm_s, stage, stage2, e00, e11,
        gxs, gxr, gys, gyr, gx_ss, gx_rs, gy_ss, gy_rs, in_sem, tab_sem, out_sem,
    ) = refs[pos : pos + 25]
    tab = dict(zip(names, refs[pos + 25 :]))
    gx = lax.axis_index("gx")
    gy = lax.axis_index("gy")

    def tab_copy(i):
        n = names[i]
        src = hbm[n]
        if n in OWN:
            src = src.at[lax.rem(gx, 2) if n == "kmask" else gy]
        return pltpu.make_async_copy(src, tab[n], tab_sem.at[i])

    waited = set()

    def need(*wanted):
        for n in wanted:
            if n not in waited:
                waited.add(n)
                tab_copy(names.index(n)).wait()
        got = tuple(tab[n][...] for n in wanted)
        return got if len(got) > 1 else got[0]

    x_in = pltpu.make_async_copy(x_hbm, x_v, in_sem.at[0])
    cot_in = pltpu.make_async_copy(cot_hbm, cot_v, in_sem.at[1])
    w_in = pltpu.make_async_copy(w_hbm, w_v, in_sem.at[2])
    x_in.start()
    for i in range(4):
        tab_copy(i).start()
    barrier = pltpu.get_barrier_semaphore()

    @pl.loop(1, GX)
    def _(o):
        pl.semaphore_signal(
            barrier, inc=1, device_id=(lax.rem(gx + o, GX), gy), device_id_type=MESH
        )

    @pl.loop(1, GY)
    def _(o):
        pl.semaphore_signal(
            barrier, inc=1, device_id=(gx, lax.rem(gy + o, GY)), device_id_type=MESH
        )

    cot_in.start()
    w_in.start()
    for i in range(4, len(names)):
        tab_copy(i).start()

    def gx_copy(step, o, landing):
        peer = lax.rem(gx + o, GX)
        return pltpu.make_async_remote_copy(
            src_ref=gxs.at[step, peer],
            dst_ref=gxr.at[step, landing],
            send_sem=gx_ss.at[step, o],
            recv_sem=gx_rs.at[step, o],
            device_id=(peer, gy),
            device_id_type=MESH,
        )

    def gy_copy(step, o, landing):
        peer = lax.rem(gy + o, GY)
        return pltpu.make_async_remote_copy(
            src_ref=gys.at[step, peer],
            dst_ref=gyr.at[step, landing],
            send_sem=gy_ss.at[step, o],
            recv_sem=gy_rs.at[step, o],
            device_id=(gx, peer),
            device_id_type=MESH,
        )

    def gx_wait(step):
        @pl.loop(1, GX)
        def _(o):
            gx_copy(step, o, lax.rem(gx + GX - o, GX)).wait_recv()

    def gy_wait(step):
        @pl.loop(1, GY)
        def _(o):
            gy_copy(step, o, lax.rem(gy + GY - o, GY)).wait_recv()

    def gy_send(step):
        @pl.loop(1, GY)
        def _(o):
            gy_copy(step, o, gy).start()

        gyr[step, gy] = gys[step, gy]

    lane = lax.broadcasted_iota(jnp.int32, (16, 128), 1)

    chan = need("chan")
    chan_f = chan.astype(F32)
    gain0 = jnp.sum(chan_f * gain_ref[0:1, :], axis=1, keepdims=True)
    gain1 = jnp.sum(chan_f * gain_ref[1:2, :], axis=1, keepdims=True)
    bias = jnp.sum(chan_f * bias_ref[...], axis=1, keepdims=True)

    for x in range(XL):
        perm_s[x * YL : (x + 1) * YL, :] = perm_ref[x]
    cell = need("cell")
    perm_hi, perm_lo = split(perm_s[...])
    col = lax.broadcasted_iota(jnp.int32, (XL * YL, 32), 0)
    cell_id = (gx * XL + col // YL) * NY + gy * YL + col % YL
    hits = (cells_ref[...] == cell_id).astype(BF)
    inflow = 0.5 * dot_nt(hits, rates_ref[...].astype(F32).astype(BF))
    perm_rows = dot(cell, perm_hi) + dot(cell, perm_lo)
    flow_rows = dot(cell, inflow.astype(BF))
    ztrep = need("ztrep")
    x_in.wait()
    ft = need("ft")

    def spread_rows(src, x, dst):
        for c in range(C):
            dst[c * YL : (c + 1) * YL, :] = src[c, x].astype(F32)

    for x in range(XL):
        rows = slice(x * CY, (x + 1) * CY)
        parts = jnp.concatenate([gain0 * perm_rows[rows], gain1 * flow_rows[rows]], axis=1)
        hi, lo = split(parts)
        added = dot(hi, ztrep) + dot(lo, ztrep)
        spread_rows(x_v, x, base.at[x])
        total = (base[x] + added).astype(BF)
        lbf[x, :CY] = total
        lbf[x, CY:] = total[:48]

    def zt_forward(field):
        for x in range(0, XL, 2):
            z = dot_nt(ft, field[x : x + 2].reshape(256, ZT))
            stage[:, x, :] = z[:, :128]
            stage[:, x + 1, :] = z[:, 128:]

    def pack(step, peer, into):
        blk = [
            stage[pl.ds((peer * ML + m) * 2, 2)].reshape(16, 128) for m in range(ML)
        ]
        for t in range(6):
            other = blk[6 + t] if t < 3 else pltpu.roll(blk[3 + t], 32, 1)
            into[:, t * 128 : (t + 1) * 128] = jnp.where(lane < 80, blk[t], other).astype(BF)

    def gx_send_packed(step):
        @pl.loop(1, GX)
        def _(o):
            peer = lax.rem(gx + o, GX)
            pack(step, peer, gxs.at[step, peer])
            gx_copy(step, o, gx).start()

        pack(step, gx, gxr.at[step, gx])

    def to_owners(step, gstep):
        got = gxr[step].reshape(256, LANES)
        xs = dot(need("wx"), got).astype(BF)
        ys = dot(xs, need("perm")).astype(BF)
        rows = jnp.concatenate(
            [ys[:, y * 256 : (y + 1) * 256] for y in range(YL)] + [jnp.zeros((64, 256), BF)], axis=0
        )
        gys[gstep] = dot(need("pick"), rows).astype(BF).reshape(GY, 16, 256)
        gy_send(gstep)

    def spectrum(gstep):
        spec = dot(need("v"), gyr[gstep].reshape(GY * 16, 256)).astype(BF)
        return jnp.concatenate([spec, jnp.zeros((80, 256), BF)], axis=0)

    def expand(spec, forms, mask, spread):
        rep = tab["rep"][forms * RB : (forms + 2) * RB, :]
        rows = dot(rep, spec).astype(BF) * jnp.concatenate([mask, mask], axis=0)
        return dot(rows, spread)

    def mixing(terms, summing, mask):
        wide = jnp.concatenate([wf[...], wf[...]], axis=0)
        rows = dot((terms * wide).astype(BF), summing).astype(BF)
        rows = rows * jnp.concatenate([mask, mask], axis=0)
        mixed = dot(need("back"), rows).astype(BF)
        return jnp.concatenate([mixed, jnp.zeros((80, 256), BF)], axis=0)

    def spread_y(gstep, mixed):
        gys[gstep] = dot(need("u"), mixed).astype(BF).reshape(GY, 16, 256)
        gy_send(gstep)

    def to_columns(gstep, step):
        ys = dot(need("sel"), gyr[gstep].reshape(GY * 16, 256)).astype(BF)
        wide = jnp.concatenate([ys[y * 48 : (y + 1) * 48] for y in range(YL)], axis=1)
        xs = dot(wide, need("perm_t")).astype(BF)
        xs = jnp.concatenate([xs, jnp.zeros((80, LANES), BF)], axis=0)
        gxs[step] = dot(need("xi"), xs).astype(BF).reshape(GX, 16, LANES)

        @pl.loop(1, GX)
        def _(o):
            gx_copy(step, o, gx).start()

        gxr[step, gx] = gxs[step, gx]

    def unpack(step, src):
        got = [gxr[step, src, :, t * 128 : (t + 1) * 128].astype(F32) for t in range(6)]
        for m in range(ML):
            if m < 6:
                v = got[m]
            else:
                v = jnp.where(
                    lane < 48, pltpu.roll(got[m - 6], 48, 1), pltpu.roll(got[m - 3], 96, 1)
                )
            stage2[pl.ds((src * ML + m) * 2, 2)] = v.reshape(2, 8, 128)

    def receive_images(step):
        unpack(step, gx)

        @pl.loop(1, GX)
        def _(o):
            src = lax.rem(gx + GX - o, GX)
            gx_copy(step, o, src).wait_recv()
            unpack(step, src)

    zt_forward(lbf)
    pl.semaphore_wait(barrier, GX + GY - 2)
    gx_send_packed(0)

    chan_t, same_y = need("chan_t", "same_y")
    pw = pw_ref[...]
    pw_fwd = (dot(dot_nt(chan, pw).astype(BF), chan_t) * same_y.astype(F32)).astype(BF)
    pw_bwd = (dot(dot(chan, pw).astype(BF), chan_t) * same_y.astype(F32)).astype(BF)
    for x in range(XL):
        base[x] = dot(pw_fwd, lbf[x]) + bias
    w_in.wait()
    wf[...] = jnp.zeros((RB, 512), F32)
    for i in range(RL * ML):
        wf[2 * i : 2 * i + 2, :400] = w_v[i].astype(F32)

    gx_wait(0)
    to_owners(0, 0)
    cot_in.wait()
    for x in range(XL):
        spread_rows(cot_v, x, cotf.at[x])
    need("rep")
    mask, spread1, sum1 = need("mask", "spread1", "sum1")
    gy_wait(0)
    spec_in = spectrum(0)
    spread_y(1, mixing(expand(spec_in, 0, mask, spread1), sum1, mask))
    kmask = need("kmask")
    both = expand(spec_in, 4, kmask, spread1)
    e00[...] = both[:RB]
    e11[...] = both[RB:]
    gy_wait(1)
    to_columns(1, 1)
    inv = need("inv")
    receive_images(1)
    for x in range(XL):
        image = dot_tn(stage2[:, x, :].astype(BF), inv)
        pre = base[x] + image[:CY]
        delta = (cotf[x] * gelu_slope(pre)).astype(BF)
        lbf[x, :CY] = delta
        lbf[x, CY:] = delta[:48]

    zt_forward(lbf)
    gx_send_packed(2)
    for x in range(XL):
        base[x] = dot(pw_bwd, lbf[x])
    spread2, sum2 = need("spread2", "sum2")
    gx_wait(2)
    to_owners(2, 2)
    gy_wait(2)
    terms = expand(spectrum(2), 2, mask, spread2)
    spread_y(3, mixing(terms, sum2, mask))
    grad = terms[:RB] * e00[...] + terms[RB:] * e11[...]
    wf[...] = grad
    for i in range(RL * ML):
        gs_v[i] = wf[2 * i : 2 * i + 2, :400]
    gs_out = pltpu.make_async_copy(gs_v, gs_hbm, out_sem.at[XL])
    gs_out.start()
    gy_wait(3)
    to_columns(3, 3)
    zsum = need("zsum")
    receive_images(3)

    def out_copy(x):
        return pltpu.make_async_copy(out_v.at[:, x], out_hbm.at[:, x], out_sem.at[x])

    for x in range(XL):
        image = dot_tn(stage2[:, x, :].astype(BF), inv)
        field = base[x] + image[:CY]
        cotf[x] = field
        for c in range(C):
            out_v[c, x] = cotf[x, c * YL : (c + 1) * YL, :].astype(BF)
        out_copy(x).start()
        hi, lo = split(field * gain0)
        zs = dot(hi, zsum) + dot(lo, zsum)
        acc = zs[:8]
        for c in range(1, CY // 8):
            acc = acc + zs[8 * c : 8 * c + 8]
        gp_ref[x] = (acc[:4] + acc[4:])[:, :NZ]

    for x in range(XL):
        out_copy(x).wait()
    gs_out.wait()
    for step in range(4):

        @pl.loop(1, GX)
        def _(o):
            gx_copy(step, o, gx).wait_send()

        @pl.loop(1, GY)
        def _(o):
            gy_copy(step, o, gy).wait_send()


def on_device(
    layer_input, cotangent, log_perm, well_cells, well_rates, inject_gain, spectral_weight,
    point_weight, point_bias,
):
    table = tables()
    weight = jnp.transpose(spectral_weight, (1, 2, 0, 3)).reshape(RL * ML, 2, C * C)
    hbm = pl.BlockSpec(memory_space=pl.ANY)
    vmem = pl.BlockSpec(memory_space=pltpu.VMEM)
    scratch = [
        pltpu.VMEM((C, XL, YL, ZT), BF),
        pltpu.VMEM((C, XL, YL, ZT), BF),
        pltpu.VMEM((RL * ML, 2, C * C), BF),
        pltpu.VMEM((C, XL, YL, ZT), BF),
        pltpu.VMEM((RL * ML, 2, C * C), F32),
        pltpu.VMEM((XL, 128, ZT), BF),
        pltpu.VMEM((XL, CY, ZT), F32),
        pltpu.VMEM((XL, CY, ZT), F32),
        pltpu.VMEM((RB, 512), F32),
        pltpu.VMEM((XL * YL, NZ), F32),
        pltpu.VMEM((NMODE, XL, 128), F32),
        pltpu.VMEM((NMODE, XL, 128), F32),
        pltpu.VMEM((RB, 512), F32),
        pltpu.VMEM((RB, 512), F32),
        pltpu.VMEM((4, GX, 16, LANES), BF),
        pltpu.VMEM((4, GX, 16, LANES), BF),
        pltpu.VMEM((4, GY, 16, 256), BF),
        pltpu.VMEM((4, GY, 16, 256), BF),
        pltpu.SemaphoreType.DMA((4, GX)),
        pltpu.SemaphoreType.DMA((4, GX)),
        pltpu.SemaphoreType.DMA((4, GY)),
        pltpu.SemaphoreType.DMA((4, GY)),
        pltpu.SemaphoreType.DMA((3,)),
        pltpu.SemaphoreType.DMA((len(TABLE_ORDER),)),
        pltpu.SemaphoreType.DMA((XL + 1,)),
    ]
    for n in TABLE_ORDER:
        shape = table[n].shape[1:] if n in OWN else table[n].shape
        scratch.append(pltpu.VMEM(shape, BF))
    grad_input, grad_spec, grad_perm = pl.pallas_call(
        kernel,
        out_shape=(
            jax.ShapeDtypeStruct((C, XL, YL, ZT), BF),
            jax.ShapeDtypeStruct((RL * ML, 2, C * C), F32),
            jax.ShapeDtypeStruct((XL, YL, NZ), F32),
        ),
        in_specs=[hbm] * 3 + [vmem] * 6 + [hbm] * len(TABLE_ORDER),
        out_specs=(hbm, hbm, vmem),
        scratch_shapes=scratch,
        compiler_params=pltpu.CompilerParams(
            collective_id=0, has_side_effects=True, vmem_limit_bytes=56 * 1024 * 1024
        ),
    )(
        layer_input, cotangent, weight, log_perm, well_cells.reshape(1, -1), well_rates.T,
        inject_gain, point_weight, point_bias.reshape(1, -1),
        *[jnp.asarray(table[n]) for n in TABLE_ORDER],
    )
    grad_spec = jnp.transpose(grad_spec.reshape(RL, ML, 2, C * C), (2, 0, 1, 3))
    return grad_input, grad_spec, grad_perm


def solution(mesh):
    return jax.shard_map(
        on_device,
        mesh=mesh,
        in_specs=(
            P(None, "gx", "gy", None),
            P(None, "gx", "gy", None),
            P("gx", "gy", None),
            P(),
            P(),
            P(),
            P(None, "gy", "gx", None),
            P(),
            P(),
        ),
        out_specs=(P(None, "gx", "gy", None), P(None, "gy", "gx", None), P("gx", "gy", None)),
        check_vma=False,
    )
```

time: 731 us -> 127 us (0.17); the launches traced: 721 us -> 126 us
  waiting for transfers between devices: 327 us -> 0 us
  local copies, waits for them, and re-layouts: 171 us -> 4.56 us
  Pallas kernels: 0 us -> 121 us
  blocking collectives: 92.7 us -> 0 us
  starting transfers between devices: 58.7 us -> 0 us
  matrix products: 41.8 us -> 0 us
  other arithmetic: 14.9 us -> 0 us
  between operations: 15.2 us -> 0.66 us
    psum x2 -> x0, waiting for transfers between devices: 299 us -> none  [spectra(): total = lax.psum(term.astype(jnp.bfloat16), 'gy').astype(jnp.float32)]
    pallas_call x0 -> x1, Pallas kernels: none -> 121 us  [on_device(): pl.pallas_call(kernel, out_shape=(jax.ShapeDtypeStruct((C, XL, YL, ZT), B...]
    all_gather x2 -> x0, blocking collectives: 75.3 us -> none  [field_of(): piece = lax.all_gather(spec, 'gy', axis=0, tiled=True)]
    all_to_all x3 -> x0, starting transfers between devices: 58 us -> none  [the longest x2 47.7 us: field_of(): lax.all_to_all(rows_out, 'gx', split_axis=2, concat_axis=3, tiled=True)]
    unnamed x51 -> x7, local copies, waits for them, and re-layouts: 53.6 us -> 4.56 us
    reshape x15 -> x0, local copies, waits for them, and re-layouts: 48 us -> none  [the longest x2 33.8 us: spectra(): depth_spec = depth_spec.reshape(2, y_cells, x_cells, MZ * MT * channels)]
    dot_general x40 -> x0, matrix products: 41.8 us -> none  [the longest x1 5.98 us: on_device(): jnp.einsum('c,cak->ak', inject_gain[0], grad_field, precision=HIGH)]
    all_to_all x3 -> x0, waiting for transfers between devices: 27.7 us -> none  [the longest x2 14.2 us: field_of(): lax.all_to_all(rows_out, 'gx', split_axis=2, concat_axis=3, tiled=True)]
  transfers between devices with their start and end apart: 5 -> 0, of which waited for: 5 -> 0; matrix products, arithmetic and copies ran while one was open for 3% -> 0% of each run, Pallas kernels for 0% -> 0%
where the time goes in v1:
time: 127 us; the launch traced here: 126 us
  Pallas kernels  121 us (95%)
  local copies, waits for them, and re-layouts  4.56 us (4%)
    pallas_call x1, Pallas kernels, on_device(): pl.pallas_call(kernel, out_shape=(jax.ShapeDtypeStruct((C, XL, YL, ZT), B...  121 us
    unnamed x7, local copies, waits for them, and re-layouts  4.56 us

profile of v1, /device:TPU:1, one launch (start us, length us, event | category | flops | bytes accessed | tf_op | source)
XLA Modules:
  0.0 126.5 jit_solution(5034675385969909952)
XLA Ops:
  0.6 121.3 %shard_map.328 = (bf16[20,8,4,1024]{3,2,1,0:T(4,128)(2,1)}, f32[162,2,400]{2,1,0:T(2,128)}, f32[8,4,64]{2,1,0:T(4,128)}) custom-call(bf16[20,8,4,1024]{3,2,1,0:T(4,128)(2,1)} %refs_0_.1, bf16[20,8,4,1024]{3,2,1,0:T(4,128)(2,1)} %refs_1_.1, bf16[162,2,400]{2,1,0:T(2,128)(2,1)} %bitcast.10, f32[8,4,64]{2,1,0:T(4,128)} %refs_3_.1, s32[1,32]{1,0:T(1,128)} %bitcast.12, ...), custom_call_target="tpu_custom_call" | custom-call | tf_op jit(solution)/shard_map/pallas_call | solution.py:536
  121.9 0.0 copy-start
  121.9 0.0 copy-start.1
  121.9 3.1 %copy.39 = bf16[20,8,4,1024]{3,2,1,0:T(4,128)(2,1)} copy(bf16[20,8,4,1024]{3,2,1,0:T(4,128)(2,1)} %get-tuple-element.12) | data formatting | bytes 2621440
  125.0 0.0 copy-done
  125.0 0.8 copy.40
  125.9 0.0 copy-done.1
  125.9 0.6 copy.41
Async XLA Ops:
  121.9 3.1 %copy-start = (f32[162,2,400]{2,1,0:T(2,128)S(1)}, f32[162,2,400]{2,1,0:T(2,128)}, u32[]{:S(2)}) copy-start(f32[162,2,400]{2,1,0:T(2,128)} %get-tuple-element.7) | copy-start | bytes 1555204
  121.9 4.0 %copy-start.1 = (f32[8,4,64]{2,1,0:T(4,128)S(1)}, f32[8,4,64]{2,1,0:T(4,128)}, u32[]{:S(2)}) copy-start(f32[8,4,64]{2,1,0:T(4,128)} %get-tuple-element.14) | copy-start | bytes 24580

commit v2 on v1

--- a/solution.py
+++ b/solution.py
@@ -19,8 +19,11 @@
 ZT = NZ * NT
 CY = C * YL
 NMODE = 2 * MZ * MT
-LANES = 768
-RB = 384
+NQ = 3
+MQ = ML // NQ
+LANES = 256
+QL = 128
+RB = 128
 BF = jnp.bfloat16
 F32 = jnp.float32
 MESH = pl.DeviceIdType.MESH
@@ -33,11 +36,18 @@
 
 
 def lane_of(m, cy):
-    if m < 6:
-        return m * 128 + cy
-    if cy < 48:
-        return (m - 6) * 128 + 80 + cy
-    return (m - 3) * 128 + 80 + cy - 48
+    if m == 0:
+        return cy
+    if m == 2:
+        return 128 + cy
+    return 80 + cy if cy < 48 else 208 + cy - 48
+
+
+X_FAR = [8] + [o for k in range(7, 0, -1) for o in (k, GX - k)]
+Y_FAR = sorted(
+    ((dz, dx) for dz in range(8) for dx in range(4) if dz or dx),
+    key=lambda d: -(min(d[0], 8 - d[0]) + min(d[1], 4 - d[1])),
+)
 
 
 def first_jx(d):
@@ -51,8 +61,13 @@
     ang = 2 * np.pi / ZT * turns
     cos, sin = np.cos(ang) / math.sqrt(ZT), np.sin(ang) / math.sqrt(ZT)
     kap = np.where(jt == 0, 1.0, 2.0)[:, None]
-    ft = np.stack([cos, -sin], 1).reshape(NMODE, ZT)
-    inv = np.stack([kap * cos, -kap * sin], 1).reshape(NMODE, ZT)
+    ft = np.stack([cos, -sin], 1)
+    inv = np.stack([kap * cos, -kap * sin], 1)
+
+    def by_chunk(a):
+        return a.reshape(GX, NQ, MQ, 2, ZT).transpose(1, 0, 2, 3, 4).reshape(NMODE, ZT)
+
+    ft, inv = by_chunk(ft), by_chunk(inv)
     jx = np.arange(MX)
     ang = 2 * np.pi / NX * (freq(jx, MX)[:, None] * np.arange(NX)[None] % NX)
     cx = (np.cos(ang) / math.sqrt(NX)).reshape(MX, GX, XL)
@@ -63,11 +78,11 @@
     wx = wx.reshape(2 * MX, 2 * NX)
     xi = np.zeros((2 * NX, 128))
     xi[:, : 2 * MX] = wx.T
-    perm = np.zeros((LANES, YL * 256))
-    for m in range(ML):
+    perm = np.zeros((LANES, YL * QL))
+    for m in range(MQ):
         for c in range(C):
             for y in range(YL):
-                perm[lane_of(m, c * YL + y), y * 256 + m * C + c] = 1
+                perm[lane_of(m, c * YL + y), y * QL + m * C + c] = 1
     pick = np.zeros((GY, YL, 2, 2, YL, MX, 2))
     for d in range(GY):
         for s in range(2):
@@ -104,21 +119,21 @@
         ((1, 1), (1, 1)),
     ]
     back = np.zeros((48, 2, RB))
-    mask = np.zeros((RB, 256))
-    kmask = np.zeros((2, RB, 256))
+    mask = np.zeros((RB, QL))
+    kmask = np.zeros((2, RB, QL))
     for r in range(RL):
-        for m in range(ML):
+        for m in range(MQ):
             for p in range(2):
-                row = (r * ML + m) * 2 + p
+                row = (r * MQ + m) * 2 + p
                 for f, form in enumerate(forms):
                     rep[f, row, 2 * r + form[p][0]] = form[p][1]
                 back[2 * r, 0, row] = 1
                 back[2 * r + 1, 1, row] = 1
                 mask[row, m * C : (m + 1) * C] = 1
                 for g in range(2):
-                    kmask[g, row, m * C : (m + 1) * C] = 1 if (ML * g + m) % MT == 0 else 2
-    spread = np.zeros((2, 256, 512))
-    for m in range(ML):
+                    kmask[g, row, m * C : (m + 1) * C] = 1 if (MQ * g + m) % MT == 0 else 2
+    spread = np.zeros((2, QL, 512))
+    for m in range(MQ):
         for c in range(C):
             for o in range(C):
                 spread[0, m * C + c, c * C + o] = 1
@@ -153,7 +168,7 @@
     "cell", "chan", "ztrep", "ft", "chan_t", "same_y", "wx", "perm", "pick", "v", "rep", "mask",
     "spread1", "sum1", "back", "u", "sel", "perm_t", "xi", "inv", "kmask", "spread2", "sum2", "zsum",
 )
-OWN = {"v": 32, "u": 32, "kmask": 2}
+OWN = ("v", "u")
 
 
 def dot(a, b):
@@ -193,10 +208,10 @@
     out_hbm, gs_hbm, gp_ref = refs[pos : pos + 3]
     pos += 3
     (
-        x_v, cot_v, w_v, out_v, gs_v, lbf, base, cotf, wf, perm_s, stage, stage2, e00, e11,
+        x_v, cot_v, w_v, out_v, gs_v, lbf, base, cotf, wf, perm_s, stage, stage2, e00, e11, grad, spec_in,
         gxs, gxr, gys, gyr, gx_ss, gx_rs, gy_ss, gy_rs, in_sem, tab_sem, out_sem,
-    ) = refs[pos : pos + 25]
-    tab = dict(zip(names, refs[pos + 25 :]))
+    ) = refs[pos : pos + 27]
+    tab = dict(zip(names, refs[pos + 27 :]))
     gx = lax.axis_index("gx")
     gy = lax.axis_index("gy")
 
@@ -204,7 +219,7 @@
         n = names[i]
         src = hbm[n]
         if n in OWN:
-            src = src.at[lax.rem(gx, 2) if n == "kmask" else gy]
+            src = src.at[gy]
         return pltpu.make_async_copy(src, tab[n], tab_sem.at[i])
 
     waited = set()
@@ -237,49 +252,42 @@
             barrier, inc=1, device_id=(gx, lax.rem(gy + o, GY)), device_id_type=MESH
         )
 
-    cot_in.start()
-    w_in.start()
-    for i in range(4, len(names)):
-        tab_copy(i).start()
-
-    def gx_copy(step, o, landing):
+    def gx_copy(step, q, o, landing):
         peer = lax.rem(gx + o, GX)
         return pltpu.make_async_remote_copy(
-            src_ref=gxs.at[step, peer],
-            dst_ref=gxr.at[step, landing],
-            send_sem=gx_ss.at[step, o],
-            recv_sem=gx_rs.at[step, o],
+            src_ref=gxs.at[step * NQ + q, peer],
+            dst_ref=gxr.at[step * NQ + q, landing],
+            send_sem=gx_ss.at[step * NQ + q],
+            recv_sem=gx_rs.at[step * NQ + q],
             device_id=(peer, gy),
             device_id_type=MESH,
         )
 
-    def gy_copy(step, o, landing):
-        peer = lax.rem(gy + o, GY)
+    def gy_copy(step, q, o, landing):
+        peer = lax.rem(gy // 4 + o[0], 8) * 4 + lax.rem(gy + o[1], 4)
         return pltpu.make_async_remote_copy(
-            src_ref=gys.at[step, peer],
-            dst_ref=gyr.at[step, landing],
-            send_sem=gy_ss.at[step, o],
-            recv_sem=gy_rs.at[step, o],
+            src_ref=gys.at[step * NQ + q, peer],
+            dst_ref=gyr.at[step * NQ + q, landing],
+            send_sem=gy_ss.at[step * NQ + q],
+            recv_sem=gy_rs.at[step * NQ + q],
             device_id=(gx, peer),
             device_id_type=MESH,
         )
 
-    def gx_wait(step):
-        @pl.loop(1, GX)
-        def _(o):
-            gx_copy(step, o, lax.rem(gx + GX - o, GX)).wait_recv()
-
-    def gy_wait(step):
-        @pl.loop(1, GY)
-        def _(o):
-            gy_copy(step, o, lax.rem(gy + GY - o, GY)).wait_recv()
-
-    def gy_send(step):
-        @pl.loop(1, GY)
-        def _(o):
-            gy_copy(step, o, gy).start()
-
-        gyr[step, gy] = gys[step, gy]
+    def all_blocks(buf, sem, i, peers):
+        blocks = buf.at[i, pl.ds(0, peers - 1)]
+        return pltpu.make_async_copy(blocks, blocks, sem.at[i])
+
+    def gx_wait(step, q):
+        all_blocks(gxr, gx_rs, step * NQ + q, GX).wait()
+
+    def gy_wait(step, q):
+        all_blocks(gyr, gy_rs, step * NQ + q, GY).wait()
+
+    def gy_send(step, q):
+        for o in Y_FAR:
+            gy_copy(step, q, o, gy).start()
+        gyr[step * NQ + q, gy] = gys[step * NQ + q, gy]
 
     lane = lax.broadcasted_iota(jnp.int32, (16, 128), 1)
 
@@ -300,8 +308,14 @@
     perm_rows = dot(cell, perm_hi) + dot(cell, perm_lo)
     flow_rows = dot(cell, inflow.astype(BF))
     ztrep = need("ztrep")
+    ft = need("ft")
     x_in.wait()
-    ft = need("ft")
+    w_in.start()
+    for i in range(4, 10):
+        tab_copy(i).start()
+    cot_in.start()
+    for i in range(10, len(names)):
+        tab_copy(i).start()
 
     def spread_rows(src, x, dst):
         for c in range(C):
@@ -323,85 +337,90 @@
             stage[:, x, :] = z[:, :128]
             stage[:, x + 1, :] = z[:, 128:]
 
-    def pack(step, peer, into):
-        blk = [
-            stage[pl.ds((peer * ML + m) * 2, 2)].reshape(16, 128) for m in range(ML)
-        ]
-        for t in range(6):
-            other = blk[6 + t] if t < 3 else pltpu.roll(blk[3 + t], 32, 1)
-            into[:, t * 128 : (t + 1) * 128] = jnp.where(lane < 80, blk[t], other).astype(BF)
+    def pack(q, peer, into):
+        row = (q * GX + peer) * MQ * 2
+        blk = [stage[pl.ds(row + 2 * m, 2)].reshape(16, 128) for m in range(MQ)]
+        into[:, :128] = jnp.where(lane < 80, blk[0], blk[1]).astype(BF)
+        into[:, 128:] = jnp.where(lane < 80, blk[2], pltpu.roll(blk[1], 32, 1)).astype(BF)
+
+    def gx_send(step, q):
+        for o in X_FAR:
+            gx_copy(step, q, o, gx).start()
+        gxr[step * NQ + q, gx] = gxs[step * NQ + q, gx]
 
     def gx_send_packed(step):
-        @pl.loop(1, GX)
-        def _(o):
-            peer = lax.rem(gx + o, GX)
-            pack(step, peer, gxs.at[step, peer])
-            gx_copy(step, o, gx).start()
-
-        pack(step, gx, gxr.at[step, gx])
-
-    def to_owners(step, gstep):
-        got = gxr[step].reshape(256, LANES)
+        for q in range(NQ):
+            for peer in range(GX):
+                pack(q, peer, gxs.at[step * NQ + q, peer])
+            gx_send(step, q)
+
+    def to_owners(step, q):
+        gx_wait(step, q)
+        got = gxr[step * NQ + q].reshape(256, LANES)
         xs = dot(need("wx"), got).astype(BF)
         ys = dot(xs, need("perm")).astype(BF)
         rows = jnp.concatenate(
-            [ys[:, y * 256 : (y + 1) * 256] for y in range(YL)] + [jnp.zeros((64, 256), BF)], axis=0
+            [ys[:, y * QL : (y + 1) * QL] for y in range(YL)] + [jnp.zeros((64, QL), BF)], axis=0
         )
-        gys[gstep] = dot(need("pick"), rows).astype(BF).reshape(GY, 16, 256)
-        gy_send(gstep)
-
-    def spectrum(gstep):
-        spec = dot(need("v"), gyr[gstep].reshape(GY * 16, 256)).astype(BF)
-        return jnp.concatenate([spec, jnp.zeros((80, 256), BF)], axis=0)
+        gys[step * NQ + q] = dot(need("pick"), rows).astype(BF).reshape(GY, 16, QL)
+        gy_send(step, q)
+
+    def spectrum(step, q):
+        gy_wait(step, q)
+        spec = dot(need("v"), gyr[step * NQ + q].reshape(GY * 16, QL)).astype(BF)
+        return jnp.concatenate([spec, jnp.zeros((80, QL), BF)], axis=0)
 
     def expand(spec, forms, mask, spread):
         rep = tab["rep"][forms * RB : (forms + 2) * RB, :]
         rows = dot(rep, spec).astype(BF) * jnp.concatenate([mask, mask], axis=0)
         return dot(rows, spread)
 
-    def mixing(terms, summing, mask):
-        wide = jnp.concatenate([wf[...], wf[...]], axis=0)
+    def mix(step, q, terms, summing):
+        mask = need("mask")
+        wide = jnp.concatenate([wf[q], wf[q]], axis=0)
         rows = dot((terms * wide).astype(BF), summing).astype(BF)
         rows = rows * jnp.concatenate([mask, mask], axis=0)
         mixed = dot(need("back"), rows).astype(BF)
-        return jnp.concatenate([mixed, jnp.zeros((80, 256), BF)], axis=0)
-
-    def spread_y(gstep, mixed):
-        gys[gstep] = dot(need("u"), mixed).astype(BF).reshape(GY, 16, 256)
-        gy_send(gstep)
-
-    def to_columns(gstep, step):
-        ys = dot(need("sel"), gyr[gstep].reshape(GY * 16, 256)).astype(BF)
+        mixed = jnp.concatenate([mixed, jnp.zeros((80, QL), BF)], axis=0)
+        gys[step * NQ + q] = dot(need("u"), mixed).astype(BF).reshape(GY, 16, QL)
+        gy_send(step, q)
+
+    def to_columns(step, q):
+        gy_wait(step, q)
+        ys = dot(need("sel"), gyr[step * NQ + q].reshape(GY * 16, QL)).astype(BF)
         wide = jnp.concatenate([ys[y * 48 : (y + 1) * 48] for y in range(YL)], axis=1)
         xs = dot(wide, need("perm_t")).astype(BF)
         xs = jnp.concatenate([xs, jnp.zeros((80, LANES), BF)], axis=0)
-        gxs[step] = dot(need("xi"), xs).astype(BF).reshape(GX, 16, LANES)
-
-        @pl.loop(1, GX)
-        def _(o):
-            gx_copy(step, o, gx).start()
-
-        gxr[step, gx] = gxs[step, gx]
-
-    def unpack(step, src):
-        got = [gxr[step, src, :, t * 128 : (t + 1) * 128].astype(F32) for t in range(6)]
-        for m in range(ML):
-            if m < 6:
-                v = got[m]
-            else:
-                v = jnp.where(
-                    lane < 48, pltpu.roll(got[m - 6], 48, 1), pltpu.roll(got[m - 3], 96, 1)
-                )
-            stage2[pl.ds((src * ML + m) * 2, 2)] = v.reshape(2, 8, 128)
-
-    def receive_images(step):
-        unpack(step, gx)
-
-        @pl.loop(1, GX)
-        def _(o):
-            src = lax.rem(gx + GX - o, GX)
-            gx_copy(step, o, src).wait_recv()
-            unpack(step, src)
+        gxs[step * NQ + q] = dot(need("xi"), xs).astype(BF).reshape(GX, 16, LANES)
+        gx_send(step, q)
+
+    def unpack(step, q, src):
+        got = [
+            gxr[step * NQ + q, src, :, t * 128 : (t + 1) * 128].astype(F32) for t in range(2)
+        ]
+        middle = jnp.where(lane < 48, pltpu.roll(got[0], 48, 1), pltpu.roll(got[1], 96, 1))
+        row = (q * GX + src) * MQ * 2
+        for m, v in enumerate((got[0], middle, got[1])):
+            stage2[row + 2 * m : row + 2 * m + 2] = v.reshape(2, 8, 128)
+
+    def receive_images(step, q):
+        gx_wait(step, q)
+        for src in range(GX):
+            unpack(step, q, src)
+
+    def exchange(step, middle, beside):
+        beside(0)
+        for q in range(NQ):
+            to_owners(step, q)
+        beside(1)
+        for q in range(NQ):
+            middle(q)
+        beside(2)
+        for q in range(NQ):
+            to_columns(step + 1, q)
+        beside(3)
+        for q in range(NQ):
+            receive_images(step + 1, q)
 
     zt_forward(lbf)
     pl.semaphore_wait(barrier, GX + GY - 2)
@@ -411,31 +430,36 @@
     pw = pw_ref[...]
     pw_fwd = (dot(dot_nt(chan, pw).astype(BF), chan_t) * same_y.astype(F32)).astype(BF)
     pw_bwd = (dot(dot(chan, pw).astype(BF), chan_t) * same_y.astype(F32)).astype(BF)
-    for x in range(XL):
-        base[x] = dot(pw_fwd, lbf[x]) + bias
-    w_in.wait()
-    wf[...] = jnp.zeros((RB, 512), F32)
-    for i in range(RL * ML):
-        wf[2 * i : 2 * i + 2, :400] = w_v[i].astype(F32)
-
-    gx_wait(0)
-    to_owners(0, 0)
-    cot_in.wait()
-    for x in range(XL):
-        spread_rows(cot_v, x, cotf.at[x])
-    need("rep")
-    mask, spread1, sum1 = need("mask", "spread1", "sum1")
-    gy_wait(0)
-    spec_in = spectrum(0)
-    spread_y(1, mixing(expand(spec_in, 0, mask, spread1), sum1, mask))
-    kmask = need("kmask")
-    both = expand(spec_in, 4, kmask, spread1)
-    e00[...] = both[:RB]
-    e11[...] = both[RB:]
-    gy_wait(1)
-    to_columns(1, 1)
+
+    def forward_middle(q):
+        spec = spectrum(0, q)
+        spec_in[q] = spec
+        mix(1, q, expand(spec, 0, need("mask"), need("spread1")), need("sum1"))
+
+    def forward_beside(slot):
+        if slot == 0:
+            need("rep")
+            w_in.wait()
+            wf[...] = jnp.zeros((NQ, RB, 512), F32)
+            for r in range(RL):
+                for m in range(ML):
+                    q, row = m // MQ, (r * MQ + m % MQ) * 2
+                    wf[q, row : row + 2, :400] = w_v[r * ML + m].astype(F32)
+            for x in range(XL):
+                base[x] = dot(pw_fwd, lbf[x]) + bias
+            cot_in.wait()
+            for x in range(XL):
+                spread_rows(cot_v, x, cotf.at[x])
+        if slot == 3:
+            need("kmask")
+            for q in range(NQ):
+                kmask = tab["kmask"][lax.rem(gx + q, 2)]
+                both = expand(spec_in[q], 4, kmask, need("spread1"))
+                e00[q] = both[:RB]
+                e11[q] = both[RB:]
+
+    exchange(0, forward_middle, forward_beside)
     inv = need("inv")
-    receive_images(1)
     for x in range(XL):
         image = dot_tn(stage2[:, x, :].astype(BF), inv)
         pre = base[x] + image[:CY]
@@ -445,24 +469,26 @@
 
     zt_forward(lbf)
     gx_send_packed(2)
-    for x in range(XL):
-        base[x] = dot(pw_bwd, lbf[x])
-    spread2, sum2 = need("spread2", "sum2")
-    gx_wait(2)
-    to_owners(2, 2)
-    gy_wait(2)
-    terms = expand(spectrum(2), 2, mask, spread2)
-    spread_y(3, mixing(terms, sum2, mask))
-    grad = terms[:RB] * e00[...] + terms[RB:] * e11[...]
-    wf[...] = grad
-    for i in range(RL * ML):
-        gs_v[i] = wf[2 * i : 2 * i + 2, :400]
     gs_out = pltpu.make_async_copy(gs_v, gs_hbm, out_sem.at[XL])
-    gs_out.start()
-    gy_wait(3)
-    to_columns(3, 3)
+
+    def backward_middle(q):
+        terms = expand(spectrum(2, q), 2, need("mask"), need("spread2"))
+        mix(3, q, terms, need("sum2"))
+        grad[q] = terms[:RB] * e00[q] + terms[RB:] * e11[q]
+
+    def backward_beside(slot):
+        if slot == 0:
+            for x in range(XL):
+                base[x] = dot(pw_bwd, lbf[x])
+        if slot == 3:
+            for r in range(RL):
+                for m in range(ML):
+                    q, row = m // MQ, (r * MQ + m % MQ) * 2
+                    gs_v[r * ML + m] = grad[q, row : row + 2, :400]
+            gs_out.start()
+
+    exchange(2, backward_middle, backward_beside)
     zsum = need("zsum")
-    receive_images(3)
 
     def out_copy(x):
         return pltpu.make_async_copy(out_v.at[:, x], out_hbm.at[:, x], out_sem.at[x])
@@ -484,15 +510,26 @@
     for x in range(XL):
         out_copy(x).wait()
     gs_out.wait()
-    for step in range(4):
-
-        @pl.loop(1, GX)
-        def _(o):
-            gx_copy(step, o, gx).wait_send()
-
-        @pl.loop(1, GY)
-        def _(o):
-            gy_copy(step, o, gy).wait_send()
+    for i in range(4 * NQ):
+        all_blocks(gxs, gx_ss, i, GX).wait()
+        all_blocks(gys, gy_ss, i, GY).wait()
+
+
+def hand_over(*refs):
+    given, result, held, (in_sem, out_sem) = refs[:3], refs[3:6], refs[6:9], refs[9:]
+    part = C // 5
+    places = [(0, pl.ds(i * part, part)) for i in range(5)] + [(1, slice(None)), (2, slice(None))]
+    ins, outs = [], []
+    for i, (a, at) in enumerate(places):
+        ins.append(pltpu.make_async_copy(given[a].at[at], held[a].at[at], in_sem.at[i]))
+        outs.append(pltpu.make_async_copy(held[a].at[at], result[a].at[at], out_sem.at[i]))
+    for c in ins:
+        c.start()
+    for a, b in zip(ins, outs):
+        a.wait()
+        b.start()
+    for c in outs:
+        c.wait()
 
 
 def on_device(
@@ -512,20 +549,22 @@
         pltpu.VMEM((XL, 128, ZT), BF),
         pltpu.VMEM((XL, CY, ZT), F32),
         pltpu.VMEM((XL, CY, ZT), F32),
-        pltpu.VMEM((RB, 512), F32),
+        pltpu.VMEM((NQ, RB, 512), F32),
         pltpu.VMEM((XL * YL, NZ), F32),
         pltpu.VMEM((NMODE, XL, 128), F32),
         pltpu.VMEM((NMODE, XL, 128), F32),
-        pltpu.VMEM((RB, 512), F32),
-        pltpu.VMEM((RB, 512), F32),
-        pltpu.VMEM((4, GX, 16, LANES), BF),
-        pltpu.VMEM((4, GX, 16, LANES), BF),
-        pltpu.VMEM((4, GY, 16, 256), BF),
-        pltpu.VMEM((4, GY, 16, 256), BF),
-        pltpu.SemaphoreType.DMA((4, GX)),
-        pltpu.SemaphoreType.DMA((4, GX)),
-        pltpu.SemaphoreType.DMA((4, GY)),
-        pltpu.SemaphoreType.DMA((4, GY)),
+        pltpu.VMEM((NQ, RB, 512), F32),
+        pltpu.VMEM((NQ, RB, 512), F32),
+        pltpu.VMEM((NQ, RB, 512), F32),
+        pltpu.VMEM((NQ, QL, QL), BF),
+        pltpu.VMEM((4 * NQ, GX, 16, LANES), BF),
+        pltpu.VMEM((4 * NQ, GX, 16, LANES), BF),
+        pltpu.VMEM((4 * NQ, GY, 16, QL), BF),
+        pltpu.VMEM((4 * NQ, GY, 16, QL), BF),
+        pltpu.SemaphoreType.DMA((4 * NQ,)),
+        pltpu.SemaphoreType.DMA((4 * NQ,)),
+        pltpu.SemaphoreType.DMA((4 * NQ,)),
+        pltpu.SemaphoreType.DMA((4 * NQ,)),
         pltpu.SemaphoreType.DMA((3,)),
         pltpu.SemaphoreType.DMA((len(TABLE_ORDER),)),
         pltpu.SemaphoreType.DMA((XL + 1,)),
@@ -533,13 +572,14 @@
     for n in TABLE_ORDER:
         shape = table[n].shape[1:] if n in OWN else table[n].shape
         scratch.append(pltpu.VMEM(shape, BF))
-    grad_input, grad_spec, grad_perm = pl.pallas_call(
+    results = (
+        jax.ShapeDtypeStruct((C, XL, YL, ZT), BF),
+        jax.ShapeDtypeStruct((RL * ML, 2, C * C), F32),
+        jax.ShapeDtypeStruct((XL, YL, NZ), F32),
+    )
+    done = pl.pallas_call(
         kernel,
-        out_shape=(
-            jax.ShapeDtypeStruct((C, XL, YL, ZT), BF),
-            jax.ShapeDtypeStruct((RL * ML, 2, C * C), F32),
-            jax.ShapeDtypeStruct((XL, YL, NZ), F32),
-        ),
+        out_shape=results,
         in_specs=[hbm] * 3 + [vmem] * 6 + [hbm] * len(TABLE_ORDER),
         out_specs=(hbm, hbm, vmem),
         scratch_shapes=scratch,
@@ -551,6 +591,15 @@
         inject_gain, point_weight, point_bias.reshape(1, -1),
         *[jnp.asarray(table[n]) for n in TABLE_ORDER],
     )
+    grad_input, grad_spec, grad_perm = pl.pallas_call(
+        hand_over,
+        out_shape=results,
+        in_specs=[hbm] * 3,
+        out_specs=(hbm, hbm, hbm),
+        scratch_shapes=[pltpu.VMEM(r.shape, r.dtype) for r in results]
+        + [pltpu.SemaphoreType.DMA((7,)), pltpu.SemaphoreType.DMA((7,))],
+        compiler_params=pltpu.CompilerParams(vmem_limit_bytes=56 * 1024 * 1024),
+    )(*done)
     grad_spec = jnp.transpose(grad_spec.reshape(RL, ML, 2, C * C), (2, 0, 1, 3))
     return grad_input, grad_spec, grad_perm
 

time: 127 us -> 98.2 us (0.77)
  Pallas kernels: 121 us -> 97.1 us
  local copies, waits for them, and re-layouts: 4.56 us -> 0 us
    pallas_call x1 -> x2, Pallas kernels: 121 us -> 97.1 us  [the longest x1 94.7 us: on_device(): pl.pallas_call(kernel, out_shape=results, in_specs=[hbm] * 3 + [vmem] * 6...]
    unnamed x7 -> x0, local copies, waits for them, and re-layouts: 4.56 us -> none
where the time goes in v2:
time: 98.2 us; the launch traced here: 97.9 us
  Pallas kernels  97.1 us (99%)
    pallas_call x1, Pallas kernels, on_device(): pl.pallas_call(kernel, out_shape=results, in_specs=[hbm] * 3 + [vmem] * 6...  94.7 us
    pallas_call x1, Pallas kernels, on_device(): pl.pallas_call(hand_over, out_shape=results, in_specs=[hbm] * 3, out_spec...  2.45 us

profile of v2, /device:TPU:1, one launch (start us, length us, event | category | flops | bytes accessed | tf_op | source)
XLA Modules:
  0.0 97.9 jit_solution(13488365673418528677)
XLA Ops:
  0.6 94.7 %shard_map.328 = (bf16[20,8,4,1024]{3,2,1,0:T(4,128)(2,1)}, f32[162,2,400]{2,1,0:T(2,128)}, f32[8,4,64]{2,1,0:T(4,128)}) custom-call(bf16[20,8,4,1024]{3,2,1,0:T(4,128)(2,1)} %refs_0_.1, bf16[20,8,4,1024]{3,2,1,0:T(4,128)(2,1)} %refs_1_.1, bf16[162,2,400]{2,1,0:T(2,128)(2,1)} %bitcast.9, f32[8,4,64]{2,1,0:T(4,128)} %refs_3_.1, s32[1,32]{1,0:T(1,128)} %bitcast.11, ...), custom_call_target="tpu_custom_call" | custom-call | tf_op jit(solution)/shard_map/pallas_call | solution.py:580
  95.3 2.5 %shard_map.329 = (bf16[20,8,4,1024]{3,2,1,0:T(4,128)(2,1)}, f32[162,2,400]{2,1,0:T(2,128)}, f32[8,4,64]{2,1,0:T(4,128)}) custom-call(bf16[20,8,4,1024]{3,2,1,0:T(4,128)(2,1)} %get-tuple-element.9.refs_0_, f32[162,2,400]{2,1,0:T(2,128)} %get-tuple-element.10.refs_1_, f32[8,4,64]{2,1,0:T(4,128)} %get-tuple-element.11.refs_2_), custom_call_target="tpu_custom_call" | custom-call | tf_op jit(solution)/shard_map/pallas_call | solution.py:594

commit v3 on v2

--- a/solution.py
+++ b/solution.py
@@ -78,22 +78,22 @@
     wx = wx.reshape(2 * MX, 2 * NX)
     xi = np.zeros((2 * NX, 128))
     xi[:, : 2 * MX] = wx.T
-    perm = np.zeros((LANES, YL * QL))
+    perm = np.zeros((LANES, 2 * QL))
     for m in range(MQ):
         for c in range(C):
             for y in range(YL):
-                perm[lane_of(m, c * YL + y), y * QL + m * C + c] = 1
-    pick = np.zeros((GY, YL, 2, 2, YL, MX, 2))
+                perm[lane_of(m, c * YL + y), y * 64 + m * C + c] = 1
+    pick = np.zeros((GY, 2, 2, 2, 2, MX, 2))
     for d in range(GY):
         for s in range(2):
             if s == 1 and d % 4 in (0, 3):
                 continue
-            for y in range(YL):
+            for y in range(2):
                 for p in range(2):
                     pick[d, y, s, p, y, first_jx(d) + s, p] = 1
-    pick = pick.reshape(GY * 16, YL * MX * 2)
-    pick_pad = np.zeros((GY * 16, 256))
-    pick_pad[:, : YL * MX * 2] = pick
+    pick = pick.reshape(GY * 8, MX * 4)
+    pick_pad = np.zeros((GY * 8, 128))
+    pick_pad[:, : MX * 4] = pick
     vc = np.zeros((GY, RL, 2, GY, YL, 2, 2))
     for d in range(GY):
         for i in range(RL):
@@ -104,11 +104,13 @@
             s = a - first_jx(d)
             vc[d, i, 0, :, :, s, 0], vc[d, i, 0, :, :, s, 1] = cy, sy
             vc[d, i, 1, :, :, s, 1], vc[d, i, 1, :, :, s, 0] = cy, -sy
-    vc = vc.reshape(GY, 2 * RL, GY * 16)
-    v_pad = np.zeros((GY, 48, GY * 16))
-    v_pad[:, : 2 * RL] = vc
-    u_pad = np.zeros((GY, GY * 16, 128))
-    u_pad[:, :, : 2 * RL] = vc.transpose(0, 2, 1)
+    vc = vc.reshape(GY, 2 * RL, GY, 2, 2, 4).transpose(0, 4, 1, 2, 3, 5)
+    vc = vc.reshape(GY, 2, 2 * RL, GY * 8)
+    v_pad = np.zeros((GY, 2, 48, GY * 8))
+    v_pad[:, :, : 2 * RL] = vc
+    v_pad = v_pad.reshape(GY, 96, GY * 8)
+    u_pad = np.zeros((GY, GY * 8, 128))
+    u_pad[:, :, :96] = v_pad.transpose(0, 2, 1)
     rep = np.zeros((6, RB, 128))
     forms = [
         ((0, 1), (1, -1)),
@@ -149,9 +151,10 @@
     chan_t[:, :CY] = chan.T
     same_y = np.zeros((CY, 128))
     same_y[:, :CY] = np.arange(CY)[:, None] % YL == np.arange(CY)[None] % YL
-    ztrep = np.zeros((NZ + NT, ZT))
-    ztrep[k // NT, k] = 1
-    ztrep[NZ + k % NT, k] = 1
+    ztrep = np.zeros((2, NZ + NT, ZT))
+    ztrep[:, k // NT, k] = 1
+    ztrep[:, NZ + k % NT, k] = 1
+    ztrep = ztrep.reshape(2 * (NZ + NT), ZT)
     zsum = np.zeros((ZT, 128))
     zsum[k, k // NT] = 1
     out = dict(
@@ -232,12 +235,18 @@
         got = tuple(tab[n][...] for n in wanted)
         return got if len(got) > 1 else got[0]
 
-    x_in = pltpu.make_async_copy(x_hbm, x_v, in_sem.at[0])
+    def x_in(x):
+        part = pl.ds(x, 2)
+        return pltpu.make_async_copy(x_hbm.at[:, part], x_v.at[:, part], in_sem.at[3 + x // 2])
+
     cot_in = pltpu.make_async_copy(cot_hbm, cot_v, in_sem.at[1])
     w_in = pltpu.make_async_copy(w_hbm, w_v, in_sem.at[2])
-    x_in.start()
-    for i in range(4):
+    for i in range(3):
         tab_copy(i).start()
+    x_in(0).start()
+    tab_copy(3).start()
+    for x in range(2, XL, 2):
+        x_in(x).start()
     barrier = pltpu.get_barrier_semaphore()
 
     @pl.loop(1, GX)
@@ -308,8 +317,34 @@
     perm_rows = dot(cell, perm_hi) + dot(cell, perm_lo)
     flow_rows = dot(cell, inflow.astype(BF))
     ztrep = need("ztrep")
-    ft = need("ft")
-    x_in.wait()
+
+    def spread_rows(src, x, dst):
+        for c in range(C):
+            dst[c * YL : (c + 1) * YL, :] = src[c, x].astype(F32)
+
+    def zt_pair(field, x):
+        z = dot_nt(need("ft"), field[x : x + 2].reshape(256, ZT))
+        stage[:, x, :] = z[:, :128]
+        stage[:, x + 1, :] = z[:, 128:]
+
+    parts = jnp.concatenate(
+        [
+            jnp.concatenate([gain0] * XL, axis=0) * perm_rows,
+            jnp.concatenate([gain1] * XL, axis=0) * flow_rows,
+        ],
+        axis=1,
+    )
+    parts = jnp.concatenate(split(parts), axis=1)
+    for x in range(XL):
+        if x % 2 == 0:
+            x_in(x).wait()
+        added = dot(parts[x * CY : (x + 1) * CY], ztrep)
+        spread_rows(x_v, x, base.at[x])
+        total = (base[x] + added).astype(BF)
+        lbf[x, :CY] = total
+        lbf[x, CY:] = total[:48]
+        if x % 2:
+            zt_pair(lbf, x - 1)
     w_in.start()
     for i in range(4, 10):
         tab_copy(i).start()
@@ -317,26 +352,6 @@
     for i in range(10, len(names)):
         tab_copy(i).start()
 
-    def spread_rows(src, x, dst):
-        for c in range(C):
-            dst[c * YL : (c + 1) * YL, :] = src[c, x].astype(F32)
-
-    for x in range(XL):
-        rows = slice(x * CY, (x + 1) * CY)
-        parts = jnp.concatenate([gain0 * perm_rows[rows], gain1 * flow_rows[rows]], axis=1)
-        hi, lo = split(parts)
-        added = dot(hi, ztrep) + dot(lo, ztrep)
-        spread_rows(x_v, x, base.at[x])
-        total = (base[x] + added).astype(BF)
-        lbf[x, :CY] = total
-        lbf[x, CY:] = total[:48]
-
-    def zt_forward(field):
-        for x in range(0, XL, 2):
-            z = dot_nt(ft, field[x : x + 2].reshape(256, ZT))
-            stage[:, x, :] = z[:, :128]
-            stage[:, x + 1, :] = z[:, 128:]
-
     def pack(q, peer, into):
         row = (q * GX + peer) * MQ * 2
         blk = [stage[pl.ds(row + 2 * m, 2)].reshape(16, 128) for m in range(MQ)]
@@ -359,15 +374,17 @@
         got = gxr[step * NQ + q].reshape(256, LANES)
         xs = dot(need("wx"), got).astype(BF)
         ys = dot(xs, need("perm")).astype(BF)
-        rows = jnp.concatenate(
-            [ys[:, y * QL : (y + 1) * QL] for y in range(YL)] + [jnp.zeros((64, QL), BF)], axis=0
-        )
-        gys[step * NQ + q] = dot(need("pick"), rows).astype(BF).reshape(GY, 16, QL)
+        rows = jnp.concatenate([ys[:, :QL], ys[:, QL:], jnp.zeros((32, QL), BF)], axis=0)
+        gys[step * NQ + q] = dot(need("pick"), rows).reshape(GY, 8, QL).astype(BF)
         gy_send(step, q)
 
+    def gy_rows(step, q):
+        gy_wait(step, q)
+        return gyr[step * NQ + q].astype(F32).reshape(GY * 8, QL).astype(BF)
+
     def spectrum(step, q):
-        gy_wait(step, q)
-        spec = dot(need("v"), gyr[step * NQ + q].reshape(GY * 16, QL)).astype(BF)
+        both = dot(need("v"), gy_rows(step, q))
+        spec = (both[:48] + pltpu.roll(both[48:], 64, 1)).astype(BF)
         return jnp.concatenate([spec, jnp.zeros((80, QL), BF)], axis=0)
 
     def expand(spec, forms, mask, spread):
@@ -380,15 +397,14 @@
         wide = jnp.concatenate([wf[q], wf[q]], axis=0)
         rows = dot((terms * wide).astype(BF), summing).astype(BF)
         rows = rows * jnp.concatenate([mask, mask], axis=0)
-        mixed = dot(need("back"), rows).astype(BF)
-        mixed = jnp.concatenate([mixed, jnp.zeros((80, QL), BF)], axis=0)
-        gys[step * NQ + q] = dot(need("u"), mixed).astype(BF).reshape(GY, 16, QL)
+        mixed = dot(need("back"), rows)
+        pair = jnp.concatenate([mixed, pltpu.roll(mixed, 64, 1), jnp.zeros((32, QL), F32)], axis=0)
+        gys[step * NQ + q] = dot(need("u"), pair.astype(BF)).reshape(GY, 8, QL).astype(BF)
         gy_send(step, q)
 
     def to_columns(step, q):
-        gy_wait(step, q)
-        ys = dot(need("sel"), gyr[step * NQ + q].reshape(GY * 16, QL)).astype(BF)
-        wide = jnp.concatenate([ys[y * 48 : (y + 1) * 48] for y in range(YL)], axis=1)
+        ys = dot(need("sel"), gy_rows(step, q)).astype(BF)
+        wide = jnp.concatenate([ys[:48], ys[48:]], axis=1)
         xs = dot(wide, need("perm_t")).astype(BF)
         xs = jnp.concatenate([xs, jnp.zeros((80, LANES), BF)], axis=0)
         gxs[step * NQ + q] = dot(need("xi"), xs).astype(BF).reshape(GX, 16, LANES)
@@ -407,6 +423,10 @@
         gx_wait(step, q)
         for src in range(GX):
             unpack(step, q, src)
+
+    def image_of(q, x):
+        rows = slice(q * 2 * ML * GX // NQ, (q + 1) * 2 * ML * GX // NQ)
+        return dot_tn(stage2[rows, x, :].astype(BF), need("inv")[rows])[:CY]
 
     def exchange(step, middle, beside):
         beside(0)
@@ -421,8 +441,10 @@
         beside(3)
         for q in range(NQ):
             receive_images(step + 1, q)
-
-    zt_forward(lbf)
+            if q < NQ - 1:
+                for x in range(XL):
+                    base[x] += image_of(q, x)
+
     pl.semaphore_wait(barrier, GX + GY - 2)
     gx_send_packed(0)
 
@@ -459,15 +481,14 @@
                 e11[q] = both[RB:]
 
     exchange(0, forward_middle, forward_beside)
-    inv = need("inv")
     for x in range(XL):
-        image = dot_tn(stage2[:, x, :].astype(BF), inv)
-        pre = base[x] + image[:CY]
+        pre = base[x] + image_of(NQ - 1, x)
         delta = (cotf[x] * gelu_slope(pre)).astype(BF)
         lbf[x, :CY] = delta
         lbf[x, CY:] = delta[:48]
-
-    zt_forward(lbf)
+        if x % 2:
+            zt_pair(lbf, x - 1)
+
     gx_send_packed(2)
     gs_out = pltpu.make_async_copy(gs_v, gs_hbm, out_sem.at[XL])
 
@@ -494,8 +515,7 @@
         return pltpu.make_async_copy(out_v.at[:, x], out_hbm.at[:, x], out_sem.at[x])
 
     for x in range(XL):
-        image = dot_tn(stage2[:, x, :].astype(BF), inv)
-        field = base[x] + image[:CY]
+        field = base[x] + image_of(NQ - 1, x)
         cotf[x] = field
         for c in range(C):
             out_v[c, x] = cotf[x, c * YL : (c + 1) * YL, :].astype(BF)
@@ -559,13 +579,13 @@
         pltpu.VMEM((NQ, QL, QL), BF),
         pltpu.VMEM((4 * NQ, GX, 16, LANES), BF),
         pltpu.VMEM((4 * NQ, GX, 16, LANES), BF),
-        pltpu.VMEM((4 * NQ, GY, 16, QL), BF),
-        pltpu.VMEM((4 * NQ, GY, 16, QL), BF),
+        pltpu.VMEM((4 * NQ, GY, 8, QL), BF),
+        pltpu.VMEM((4 * NQ, GY, 8, QL), BF),
         pltpu.SemaphoreType.DMA((4 * NQ,)),
         pltpu.SemaphoreType.DMA((4 * NQ,)),
         pltpu.SemaphoreType.DMA((4 * NQ,)),
         pltpu.SemaphoreType.DMA((4 * NQ,)),
-        pltpu.SemaphoreType.DMA((3,)),
+        pltpu.SemaphoreType.DMA((3 + XL // 2,)),
         pltpu.SemaphoreType.DMA((len(TABLE_ORDER),)),
         pltpu.SemaphoreType.DMA((XL + 1,)),
     ]

time: 98.2 us -> 90.8 us (0.925)
  Pallas kernels: 97.1 us -> 89.8 us
    pallas_call x1, Pallas kernels: 94.7 us -> 87.3 us  [on_device(): pl.pallas_call(kernel, out_shape=results, in_specs=[hbm] * 3 + [vmem] * 6...]
where the time goes in v3:
time: 90.8 us; the launch traced here: 90.6 us
  Pallas kernels  89.8 us (99%)
    pallas_call x1, Pallas kernels, on_device(): pl.pallas_call(kernel, out_shape=results, in_specs=[hbm] * 3 + [vmem] * 6...  87.3 us
    pallas_call x1, Pallas kernels, on_device(): pl.pallas_call(hand_over, out_shape=results, in_specs=[hbm] * 3, out_spec...  2.45 us

profile of v3, /device:TPU:1, one launch (start us, length us, event | category | flops | bytes accessed | tf_op | source)
XLA Modules:
  0.0 90.6 jit_solution(4656908463851001337)
XLA Ops:
  0.6 87.3 %shard_map.328 = (bf16[20,8,4,1024]{3,2,1,0:T(4,128)(2,1)}, f32[162,2,400]{2,1,0:T(2,128)}, f32[8,4,64]{2,1,0:T(4,128)}) custom-call(bf16[20,8,4,1024]{3,2,1,0:T(4,128)(2,1)} %refs_0_.1, bf16[20,8,4,1024]{3,2,1,0:T(4,128)(2,1)} %refs_1_.1, bf16[162,2,400]{2,1,0:T(2,128)(2,1)} %bitcast.9, f32[8,4,64]{2,1,0:T(4,128)} %refs_3_.1, s32[1,32]{1,0:T(1,128)} %bitcast.11, ...), custom_call_target="tpu_custom_call" | custom-call | tf_op jit(solution)/shard_map/pallas_call | solution.py:600
  87.9 2.5 %shard_map.329 = (bf16[20,8,4,1024]{3,2,1,0:T(4,128)(2,1)}, f32[162,2,400]{2,1,0:T(2,128)}, f32[8,4,64]{2,1,0:T(4,128)}) custom-call(bf16[20,8,4,1024]{3,2,1,0:T(4,128)(2,1)} %get-tuple-element.9.refs_0_, f32[162,2,400]{2,1,0:T(2,128)} %get-tuple-element.10.refs_1_, f32[8,4,64]{2,1,0:T(4,128)} %get-tuple-element.11.refs_2_), custom_call_target="tpu_custom_call" | custom-call | tf_op jit(solution)/shard_map/pallas_call | solution.py:614

commit v4 on v3

--- a/solution.py
+++ b/solution.py
@@ -205,16 +205,19 @@
 
 def kernel(*refs):
     names = TABLE_ORDER
-    (x_hbm, cot_hbm, w_hbm, perm_ref, cells_ref, rates_ref, gain_ref, pw_ref, bias_ref) = refs[:9]
+    x_hbm, cot_hbm, w_hbm = refs[:3]
+    small_hbm = refs[3:9]
     hbm = dict(zip(names, refs[9 : 9 + len(names)]))
     pos = 9 + len(names)
-    out_hbm, gs_hbm, gp_ref = refs[pos : pos + 3]
+    out_hbm, gs_hbm, gp_hbm = refs[pos : pos + 3]
     pos += 3
     (
         x_v, cot_v, w_v, out_v, gs_v, lbf, base, cotf, wf, perm_s, stage, stage2, e00, e11, grad, spec_in,
         gxs, gxr, gys, gyr, gx_ss, gx_rs, gy_ss, gy_rs, in_sem, tab_sem, out_sem,
-    ) = refs[pos : pos + 27]
-    tab = dict(zip(names, refs[pos + 27 :]))
+        gp_ref, perm_ref, cells_ref, rates_ref, gain_ref, pw_ref, bias_ref, small_sem,
+    ) = refs[pos : pos + 35]
+    small = (perm_ref, cells_ref, rates_ref, gain_ref, pw_ref, bias_ref)
+    tab = dict(zip(names, refs[pos + 35 :]))
     gx = lax.axis_index("gx")
     gy = lax.axis_index("gy")
 
@@ -241,6 +244,12 @@
 
     cot_in = pltpu.make_async_copy(cot_hbm, cot_v, in_sem.at[1])
     w_in = pltpu.make_async_copy(w_hbm, w_v, in_sem.at[2])
+    small_in = [
+        pltpu.make_async_copy(a, b, small_sem.at[i])
+        for i, (a, b) in enumerate(zip(small_hbm, small))
+    ]
+    for c in small_in:
+        c.start()
     for i in range(3):
         tab_copy(i).start()
     x_in(0).start()
@@ -300,6 +309,8 @@
 
     lane = lax.broadcasted_iota(jnp.int32, (16, 128), 1)
 
+    for c in small_in:
+        c.wait()
     chan = need("chan")
     chan_f = chan.astype(F32)
     gain0 = jnp.sum(chan_f * gain_ref[0:1, :], axis=1, keepdims=True)
@@ -512,41 +523,48 @@
     zsum = need("zsum")
 
     def out_copy(x):
-        return pltpu.make_async_copy(out_v.at[:, x], out_hbm.at[:, x], out_sem.at[x])
+        return pltpu.make_async_copy(out_v.at[x], out_hbm.at[x], out_sem.at[x])
 
     for x in range(XL):
         field = base[x] + image_of(NQ - 1, x)
-        cotf[x] = field
-        for c in range(C):
-            out_v[c, x] = cotf[x, c * YL : (c + 1) * YL, :].astype(BF)
+        out_v[x] = field.astype(BF)
         out_copy(x).start()
-        hi, lo = split(field * gain0)
-        zs = dot(hi, zsum) + dot(lo, zsum)
+        zs = dot((field * gain0).astype(BF), zsum)
         acc = zs[:8]
         for c in range(1, CY // 8):
             acc = acc + zs[8 * c : 8 * c + 8]
         gp_ref[x] = (acc[:4] + acc[4:])[:, :NZ]
 
+    gp_out = pltpu.make_async_copy(gp_ref, gp_hbm, out_sem.at[XL + 1])
+    gp_out.start()
     for x in range(XL):
         out_copy(x).wait()
     gs_out.wait()
+    gp_out.wait()
     for i in range(4 * NQ):
         all_blocks(gxs, gx_ss, i, GX).wait()
         all_blocks(gys, gy_ss, i, GY).wait()
 
 
 def hand_over(*refs):
-    given, result, held, (in_sem, out_sem) = refs[:3], refs[3:6], refs[6:9], refs[9:]
-    part = C // 5
-    places = [(0, pl.ds(i * part, part)) for i in range(5)] + [(1, slice(None)), (2, slice(None))]
-    ins, outs = [], []
-    for i, (a, at) in enumerate(places):
-        ins.append(pltpu.make_async_copy(given[a].at[at], held[a].at[at], in_sem.at[i]))
-        outs.append(pltpu.make_async_copy(held[a].at[at], result[a].at[at], out_sem.at[i]))
+    given, result, held = refs[:3], refs[3:6], refs[6:9]
+    rows, wide, in_sem, out_sem = refs[9:]
+    ins = [pltpu.make_async_copy(given[0].at[x], rows.at[x], in_sem.at[x]) for x in range(XL)]
+    outs = [
+        pltpu.make_async_copy(held[0].at[:, x], result[0].at[:, x], out_sem.at[x])
+        for x in range(XL)
+    ]
+    for a in (1, 2):
+        ins.append(pltpu.make_async_copy(given[a], held[a], in_sem.at[XL + a - 1]))
+        outs.append(pltpu.make_async_copy(held[a], result[a], out_sem.at[XL + a - 1]))
     for c in ins:
         c.start()
-    for a, b in zip(ins, outs):
+    for i, (a, b) in enumerate(zip(ins, outs)):
         a.wait()
+        if i < XL:
+            wide[i] = rows[i].astype(F32)
+            for c in range(C):
+                held[0][c, i] = wide[i, c * YL : (c + 1) * YL, :].astype(BF)
         b.start()
     for c in outs:
         c.wait()
@@ -559,12 +577,11 @@
     table = tables()
     weight = jnp.transpose(spectral_weight, (1, 2, 0, 3)).reshape(RL * ML, 2, C * C)
     hbm = pl.BlockSpec(memory_space=pl.ANY)
-    vmem = pl.BlockSpec(memory_space=pltpu.VMEM)
     scratch = [
         pltpu.VMEM((C, XL, YL, ZT), BF),
         pltpu.VMEM((C, XL, YL, ZT), BF),
         pltpu.VMEM((RL * ML, 2, C * C), BF),
-        pltpu.VMEM((C, XL, YL, ZT), BF),
+        pltpu.VMEM((XL, CY, ZT), BF),
         pltpu.VMEM((RL * ML, 2, C * C), F32),
         pltpu.VMEM((XL, 128, ZT), BF),
         pltpu.VMEM((XL, CY, ZT), F32),
@@ -587,7 +604,15 @@
         pltpu.SemaphoreType.DMA((4 * NQ,)),
         pltpu.SemaphoreType.DMA((3 + XL // 2,)),
         pltpu.SemaphoreType.DMA((len(TABLE_ORDER),)),
-        pltpu.SemaphoreType.DMA((XL + 1,)),
+        pltpu.SemaphoreType.DMA((XL + 2,)),
+        pltpu.VMEM((XL, YL, NZ), F32),
+        pltpu.VMEM((XL, YL, NZ), F32),
+        pltpu.VMEM((1, well_cells.shape[0]), jnp.int32),
+        pltpu.VMEM(well_rates.shape[::-1], jnp.int32),
+        pltpu.VMEM((2, C), F32),
+        pltpu.VMEM((C, C), BF),
+        pltpu.VMEM((1, C), F32),
+        pltpu.SemaphoreType.DMA((6,)),
     ]
     for n in TABLE_ORDER:
         shape = table[n].shape[1:] if n in OWN else table[n].shape
@@ -599,9 +624,9 @@
     )
     done = pl.pallas_call(
         kernel,
-        out_shape=results,
-        in_specs=[hbm] * 3 + [vmem] * 6 + [hbm] * len(TABLE_ORDER),
-        out_specs=(hbm, hbm, vmem),
+        out_shape=(jax.ShapeDtypeStruct((XL, CY, ZT), BF),) + results[1:],
+        in_specs=[hbm] * (9 + len(TABLE_ORDER)),
+        out_specs=(hbm, hbm, hbm),
         scratch_shapes=scratch,
         compiler_params=pltpu.CompilerParams(
             collective_id=0, has_side_effects=True, vmem_limit_bytes=56 * 1024 * 1024
@@ -617,7 +642,12 @@
         in_specs=[hbm] * 3,
         out_specs=(hbm, hbm, hbm),
         scratch_shapes=[pltpu.VMEM(r.shape, r.dtype) for r in results]
-        + [pltpu.SemaphoreType.DMA((7,)), pltpu.SemaphoreType.DMA((7,))],
+        + [
+            pltpu.VMEM((XL, CY, ZT), BF),
+            pltpu.VMEM((XL, CY, ZT), F32),
+            pltpu.SemaphoreType.DMA((XL + 2,)),
+            pltpu.SemaphoreType.DMA((XL + 2,)),
+        ],
         compiler_params=pltpu.CompilerParams(vmem_limit_bytes=56 * 1024 * 1024),
     )(*done)
     grad_spec = jnp.transpose(grad_spec.reshape(RL, ML, 2, C * C), (2, 0, 1, 3))

time: 90.8 us -> 89.2 us (0.982)
  Pallas kernels: 89.8 us -> 88.2 us
    pallas_call x1, Pallas kernels: 87.3 us -> 85.6 us  [on_device(): pl.pallas_call(kernel, out_shape=(jax.ShapeDtypeStruct((XL, CY, ZT), BF),...]
where the time goes in v4:
time: 89.2 us; the launch traced here: 89 us
  Pallas kernels  88.2 us (99%)
    pallas_call x1, Pallas kernels, on_device(): pl.pallas_call(kernel, out_shape=(jax.ShapeDtypeStruct((XL, CY, ZT), BF),...  85.6 us
    pallas_call x1, Pallas kernels, on_device(): pl.pallas_call(hand_over, out_shape=results, in_specs=[hbm] * 3, out_spec...  2.63 us

profile of v4, /device:TPU:1, one launch (start us, length us, event | category | flops | bytes accessed | tf_op | source)
XLA Modules:
  0.0 89.0 jit_solution(12236790588851636060)
XLA Ops:
  0.6 85.6 %shard_map.328 = (bf16[8,80,1024]{2,1,0:T(8,128)(2,1)}, f32[162,2,400]{2,1,0:T(2,128)}, f32[8,4,64]{2,1,0:T(4,128)}) custom-call(bf16[20,8,4,1024]{3,2,1,0:T(4,128)(2,1)} %refs_0_.1, bf16[20,8,4,1024]{3,2,1,0:T(4,128)(2,1)} %refs_1_.1, bf16[162,2,400]{2,1,0:T(2,128)(2,1)} %bitcast.9, f32[8,4,64]{2,1,0:T(4,128)} %refs_3_.1, s32[1,32]{1,0:T(1,128)} %bitcast.11, ...), custom_call_target="tpu_custom_call" | custom-call | tf_op jit(solution)/shard_map/pallas_call | solution.py:625
  86.3 2.6 %shard_map.329 = (bf16[20,8,4,1024]{3,2,1,0:T(4,128)(2,1)}, f32[162,2,400]{2,1,0:T(2,128)}, f32[8,4,64]{2,1,0:T(4,128)}) custom-call(bf16[8,80,1024]{2,1,0:T(8,128)(2,1)} %get-tuple-element.9.refs_0_, f32[162,2,400]{2,1,0:T(2,128)} %get-tuple-element.10.refs_1_, f32[8,4,64]{2,1,0:T(4,128)} %get-tuple-element.11.refs_2_), custom_call_target="tpu_custom_call" | custom-call | tf_op jit(solution)/shard_map/pallas_call | solution.py:639

commit v5 on v4

--- a/solution.py
+++ b/solution.py
@@ -76,8 +76,6 @@
     wx[:, 0, :, 0], wx[:, 0, :, 1] = cx, sx
     wx[:, 1, :, 1], wx[:, 1, :, 0] = cx, -sx
     wx = wx.reshape(2 * MX, 2 * NX)
-    xi = np.zeros((2 * NX, 128))
-    xi[:, : 2 * MX] = wx.T
     perm = np.zeros((LANES, 2 * QL))
     for m in range(MQ):
         for c in range(C):
@@ -92,8 +90,7 @@
                 for p in range(2):
                     pick[d, y, s, p, y, first_jx(d) + s, p] = 1
     pick = pick.reshape(GY * 8, MX * 4)
-    pick_pad = np.zeros((GY * 8, 128))
-    pick_pad[:, : MX * 4] = pick
+    wx = pick.reshape(GY * 8, 2, 2 * MX).sum(1) @ wx
     vc = np.zeros((GY, RL, 2, GY, YL, 2, 2))
     for d in range(GY):
         for i in range(RL):
@@ -158,7 +155,7 @@
     zsum = np.zeros((ZT, 128))
     zsum[k, k // NT] = 1
     out = dict(
-        ft=ft, inv=inv, wx=wx, xi=xi, perm=perm, perm_t=perm.T, pick=pick_pad, sel=pick.T,
+        ft=ft, inv=inv, wx=wx, xi=wx.T, perm=perm, perm_t=perm.T,
         v=v_pad, u=u_pad, rep=rep.reshape(6 * RB, 128), back=back.reshape(48, 2 * RB),
         mask=mask, kmask=kmask, spread1=spread[0], spread2=spread[1],
         sum1=spread[1].T, sum2=spread[0].T, cell=cell, chan=chan, chan_t=chan_t,
@@ -168,8 +165,8 @@
 
 
 TABLE_ORDER = (
-    "cell", "chan", "ztrep", "ft", "chan_t", "same_y", "wx", "perm", "pick", "v", "rep", "mask",
-    "spread1", "sum1", "back", "u", "sel", "perm_t", "xi", "inv", "kmask", "spread2", "sum2", "zsum",
+    "cell", "chan", "ztrep", "ft", "chan_t", "same_y", "wx", "perm", "v", "rep", "mask",
+    "spread1", "sum1", "back", "u", "perm_t", "xi", "inv", "kmask", "spread2", "sum2", "zsum",
 )
 OWN = ("v", "u")
 
@@ -308,6 +305,7 @@
         gyr[step * NQ + q, gy] = gys[step * NQ + q, gy]
 
     lane = lax.broadcasted_iota(jnp.int32, (16, 128), 1)
+    first_pair = lax.broadcasted_iota(jnp.int32, (GY * 8, QL), 0) % 8 < 4
 
     for c in small_in:
         c.wait()
@@ -357,10 +355,10 @@
         if x % 2:
             zt_pair(lbf, x - 1)
     w_in.start()
-    for i in range(4, 10):
+    for i in range(4, 9):
         tab_copy(i).start()
     cot_in.start()
-    for i in range(10, len(names)):
+    for i in range(9, len(names)):
         tab_copy(i).start()
 
     def pack(q, peer, into):
@@ -384,9 +382,9 @@
         gx_wait(step, q)
         got = gxr[step * NQ + q].reshape(256, LANES)
         xs = dot(need("wx"), got).astype(BF)
-        ys = dot(xs, need("perm")).astype(BF)
-        rows = jnp.concatenate([ys[:, :QL], ys[:, QL:], jnp.zeros((32, QL), BF)], axis=0)
-        gys[step * NQ + q] = dot(need("pick"), rows).reshape(GY, 8, QL).astype(BF)
+        ys = dot(xs, need("perm"))
+        rows = jnp.where(first_pair, ys[:, :QL], ys[:, QL:])
+        gys[step * NQ + q] = rows.reshape(GY, 8, QL).astype(BF)
         gy_send(step, q)
 
     def gy_rows(step, q):
@@ -414,10 +412,12 @@
         gy_send(step, q)
 
     def to_columns(step, q):
-        ys = dot(need("sel"), gy_rows(step, q)).astype(BF)
-        wide = jnp.concatenate([ys[:48], ys[48:]], axis=1)
-        xs = dot(wide, need("perm_t")).astype(BF)
-        xs = jnp.concatenate([xs, jnp.zeros((80, LANES), BF)], axis=0)
+        gy_wait(step, q)
+        rows = gyr[step * NQ + q].astype(F32).reshape(GY * 8, QL)
+        wide = jnp.concatenate(
+            [jnp.where(first_pair, rows, 0.0), jnp.where(first_pair, 0.0, rows)], axis=1
+        )
+        xs = dot(wide.astype(BF), need("perm_t")).astype(BF)
         gxs[step * NQ + q] = dot(need("xi"), xs).astype(BF).reshape(GX, 16, LANES)
         gx_send(step, q)
 

time: 89.2 us -> 88.6 us (level)
  no operation moved by 1% of the time
where the time goes in v5:
time: 88.6 us; the launch traced here: 88.4 us
  Pallas kernels  87.6 us (99%)
    pallas_call x1, Pallas kernels, on_device(): pl.pallas_call(kernel, out_shape=(jax.ShapeDtypeStruct((XL, CY, ZT), BF),...  85 us
    pallas_call x1, Pallas kernels, on_device(): pl.pallas_call(hand_over, out_shape=results, in_specs=[hbm] * 3, out_spec...  2.63 us

profile of v5, /device:TPU:1, one launch (start us, length us, event | category | flops | bytes accessed | tf_op | source)
XLA Modules:
  0.0 88.4 jit_solution(6344573984426559399)
XLA Ops:
  0.6 85.0 %shard_map.310 = (bf16[8,80,1024]{2,1,0:T(8,128)(2,1)}, f32[162,2,400]{2,1,0:T(2,128)}, f32[8,4,64]{2,1,0:T(4,128)}) custom-call(bf16[20,8,4,1024]{3,2,1,0:T(4,128)(2,1)} %refs_0_.1, bf16[20,8,4,1024]{3,2,1,0:T(4,128)(2,1)} %refs_1_.1, bf16[162,2,400]{2,1,0:T(2,128)(2,1)} %bitcast.9, f32[8,4,64]{2,1,0:T(4,128)} %refs_3_.1, s32[1,32]{1,0:T(1,128)} %bitcast.11, ...), custom_call_target="tpu_custom_call" | custom-call | tf_op jit(solution)/shard_map/pallas_call | solution.py:625
  85.6 2.6 %shard_map.311 = (bf16[20,8,4,1024]{3,2,1,0:T(4,128)(2,1)}, f32[162,2,400]{2,1,0:T(2,128)}, f32[8,4,64]{2,1,0:T(4,128)}) custom-call(bf16[8,80,1024]{2,1,0:T(8,128)(2,1)} %get-tuple-element.9.refs_0_, f32[162,2,400]{2,1,0:T(2,128)} %get-tuple-element.10.refs_1_, f32[8,4,64]{2,1,0:T(4,128)} %get-tuple-element.11.refs_2_), custom_call_target="tpu_custom_call" | custom-call | tf_op jit(solution)/shard_map/pallas_call | solution.py:639
